TPU v7x, 128 devices: a whole 4x4x4 slice. The times are simulated.
128 devices in a mesh: fsdp: 32 (over z, x_hi, y), cp: 4 (over x_lo, core).
Axes of the slice: x: 4 (x_hi: 2, x_lo: 2; x = x_hi * 2 + x_lo), y: 4, z: 4, core: 2. Of those that a mesh axis runs over, the one named last changes fastest.
Arguments:
- video: bfloat16 [384, 4, 96, 512], P('fsdp', None, 'cp'), may hold values from -6 to 6
- conv_weight: bfloat16 [3, 3, 512, 512], replicated, may hold values from -0.09375 to 0.09375
- conv_bias: float32 [512], replicated, may hold values from -3 to 3
- time_weight: bfloat16 [3, 512, 512], replicated, may hold values from -0.15625 to 0.15625
- time_bias: float32 [512], replicated, may hold values from -3 to 3
- latent_weight: bfloat16 [512, 16], replicated, may hold values from -0.25 to 0.25
- latent_bias: float32 [16], replicated, may hold values from -3 to 3
- patch_weight: bfloat16 [64, 6144], replicated, may hold values from -0.75 to 0.75
- patch_bias: float32 [6144], replicated, may hold values from -3 to 3
- frame_pos: bfloat16 [8, 6144], replicated, may hold values from -3 to 3
- row_pos: bfloat16 [48, 6144], replicated, may hold values from -3 to 3
- col_pos: bfloat16 [48, 6144], replicated, may hold values from -3 to 3
- modulation: float32 [2, 6144], replicated, may hold values from -2 to 2
- qkv_weight: bfloat16 [3, 6144, 3072], P(None, 'fsdp', 'cp'), may hold values from -0.078125 to 0.078125
- qk_gain: float32 [2, 3072], P(None, 'cp'), may hold values from 0.1 to 1.9
Outputs:
- query: bfloat16 [18432, 3072], P('fsdp', 'cp')
- keys: bfloat16 [18432, 3072], P('fsdp', 'cp')
- values: bfloat16 [18432, 3072], P('fsdp', 'cp')
All inputs are finite; a program needn't handle non-finite values.
Results may differ from a plain program's by a relative error of at most 0.008.
Values may be sent and summed in bfloat16 or wider, within the bound.
A program may use at most 256 MiB of HBM per device.

v0:
```python
import jax
import jax.numpy as jnp
from jax import lax
from jax.sharding import PartitionSpec as P

D = 6144
HD = 128
C = 512
LAT = 16
FR = 4
H = 96
ROW_SPLIT = 2
COL_SPLIT = 4
WIN_SETS = 1


def padded_2(cells, sides, width):
    for axis, dim in sides:
        count = lax.axis_size(axis)
        head = lax.slice_in_dim(cells, 0, width, axis=dim)
        tail = lax.slice_in_dim(cells, cells.shape[dim] - width, cells.shape[dim], axis=dim)
        cells = jnp.concatenate(
            [
                lax.ppermute(tail, axis, [(i, (i + 1) % count) for i in range(count)]),
                cells,
                lax.ppermute(head, axis, [((i + 1) % count, i) for i in range(count)]),
            ],
            axis=dim,
        )
    return cells


def head_norm(projected_part, gain_row):
    count = projected_part.shape[0]
    shaped = projected_part.reshape(count, -1, HD)
    scale = lax.rsqrt(jnp.mean(shaped * shaped, axis=-1, keepdims=True) + 1e-06)
    return ((shaped * scale).reshape(count, -1) * gain_row).astype(jnp.bfloat16)


def embed_tokens(
    patch_block, col_table, row_table, window_table, patch_weight, patch_bias, modulation
):
    pieces = col_table.shape[0]
    base = jnp.dot(patch_block, patch_weight, preferred_element_type=jnp.float32) + patch_bias
    grid = base.reshape(
        pieces,
        window_table.shape[0],
        window_table.shape[1],
        row_table.shape[0],
        row_table.shape[1],
        col_table.shape[1],
        D,
    )
    grid = grid + window_table.astype(jnp.float32)[None, :, :, None, None, None, :]
    grid = grid + row_table.astype(jnp.float32)[None, None, None, :, :, None, :]
    grid = grid + col_table.astype(jnp.float32)[:, None, None, None, None, :, :]
    center = jnp.mean(grid, axis=-1, keepdims=True)
    spread = jnp.mean((grid - center) ** 2, axis=-1, keepdims=True)
    scale_part = 1.0 + modulation[0]
    shift_part = modulation[1]
    normed = (grid - center) * lax.rsqrt(spread + 1e-06) * scale_part + shift_part
    return normed.astype(jnp.bfloat16).reshape(-1, D)


def body(
    video,
    conv_weight,
    conv_bias,
    time_weight,
    time_bias,
    latent_weight,
    latent_bias,
    patch_weight,
    patch_bias,
    frame_pos,
    row_pos,
    col_pos,
    modulation,
    qkv_weight,
    qk_gain,
):
    fsdp_count = lax.axis_size("fsdp")
    cp_count = lax.axis_size("cp")
    position = lax.axis_index("fsdp")
    column = lax.axis_index("cp")
    block_rows = video.shape[0]
    window_count = video.shape[1]
    col_block = video.shape[2]
    row_blocks = H // block_rows
    half_blocks = row_blocks // 2
    block_index = (position + row_blocks - half_blocks) % row_blocks
    active = jax.nn.silu(video.astype(jnp.float32)).astype(jnp.bfloat16)
    padded = padded_2(active, (("fsdp", 0), ("cp", 2)), 1)
    row_ids = lax.broadcasted_iota(jnp.int32, (block_rows + 2, 1, 1, 1), 0)
    col_ids = lax.broadcasted_iota(jnp.int32, (1, 1, col_block + 2, 1), 2)
    dropped_rows = (row_ids == 0) & (block_index == 0) | (row_ids == block_rows + 1) & (
        block_index == row_blocks - 1
    )
    dropped_cols = (col_ids == 0) & (column == 0) | (col_ids == col_block + 1) & (
        column == cp_count - 1
    )
    padded = jnp.where(dropped_rows | dropped_cols, jnp.zeros((), jnp.bfloat16), padded)
    running = video.astype(jnp.float32) + conv_bias
    for row_shift in range(3):
        for col_shift in range(3):
            region = padded[
                row_shift : row_shift + block_rows, :, col_shift : col_shift + col_block, :
            ]
            running = running + jnp.dot(
                region, conv_weight[row_shift, col_shift], preferred_element_type=jnp.float32
            )
    spatial = running.astype(jnp.bfloat16)
    sub_rows = block_rows // ROW_SPLIT
    sub_cols = col_block // COL_SPLIT
    groups = window_count // WIN_SETS
    outgoing = spatial.reshape(ROW_SPLIT, sub_rows, groups, WIN_SETS, COL_SPLIT, sub_cols, C)
    outgoing = outgoing.transpose(2, 0, 4, 1, 3, 5, 6).reshape(
        fsdp_count, sub_rows, WIN_SETS, sub_cols, C
    )
    tiles = lax.all_to_all(outgoing, "fsdp", split_axis=0, concat_axis=0, tiled=True)
    tiles = jnp.roll(tiles, -half_blocks, axis=0)
    tiles = tiles.reshape(FR, row_blocks, sub_rows, WIN_SETS, sub_cols, C)
    latents = []
    for latent_frame in range(FR // 2):
        mixed = jnp.zeros((row_blocks, sub_rows, WIN_SETS, sub_cols, C), jnp.float32) + time_bias
        for offset in range(3):
            source = 2 * latent_frame + offset - 1
            if 0 <= source < FR:
                mixed = mixed + jnp.dot(
                    tiles[source], time_weight[offset], preferred_element_type=jnp.float32
                )
        mixed = mixed.astype(jnp.bfloat16)
        latents.append(
            jnp.dot(mixed, latent_weight, preferred_element_type=jnp.float32) + latent_bias
        )
    latent = jnp.stack(latents, axis=0)
    half_rows = sub_rows // 2
    half_cols = sub_cols // 2
    patches = latent.reshape(FR // 2, row_blocks, half_rows, 2, WIN_SETS, half_cols, 2, LAT)
    patches = patches.transpose(4, 0, 1, 2, 5, 3, 6, 7).reshape(-1, 4 * LAT).astype(jnp.bfloat16)
    row_part = position // COL_SPLIT % ROW_SPLIT
    col_part = position % COL_SPLIT
    group_index = position // (ROW_SPLIT * COL_SPLIT)
    row_table = lax.dynamic_index_in_dim(
        row_pos.reshape(row_blocks, ROW_SPLIT, half_rows, D), row_part, 1, False
    )
    col_tables = lax.dynamic_index_in_dim(
        col_pos.reshape(cp_count, COL_SPLIT, half_cols, D), col_part, 1, False
    )
    window_table = lax.dynamic_slice_in_dim(
        frame_pos.reshape(-1, FR // 2, D), group_index * WIN_SETS, WIN_SETS, 0
    )
    own_table = lax.dynamic_slice_in_dim(col_tables, column, 1, 0)
    local_rows = embed_tokens(
        patches, own_table, row_table, window_table, patch_weight, patch_bias, modulation
    )
    normed = lax.all_gather(local_rows, "cp", axis=0, tiled=True)
    projected = jnp.einsum(
        "tr,krh->kth",
        normed,
        lax.all_gather(qkv_weight, "fsdp", axis=1, tiled=True),
        preferred_element_type=jnp.float32,
    )
    query = head_norm(projected[0], qk_gain[0])
    keys = head_norm(projected[1], qk_gain[1])
    values = projected[2].astype(jnp.bfloat16)
    return (query, keys, values)


def solution(mesh):
    return jax.shard_map(
        body,
        mesh=mesh,
        in_specs=(
            P("fsdp", None, "cp", None),
            P(),
            P(),
            P(),
            P(),
            P(),
            P(),
            P(),
            P(),
            P(),
            P(),
            P(),
            P(),
            P(None, "fsdp", "cp"),
            P(None, "cp"),
        ),
        out_specs=(P("fsdp", "cp"), P("fsdp", "cp"), P("fsdp", "cp")),
        check_vma=False,
    )
```

profile of v0, /device:TPU:0, one launch (start us, length us, event | category | flops | bytes accessed | tf_op | source)
XLA Modules:
  0.0 469.0 jit_solution(4160187699555123217)
XLA Ops:
  7.2 2.1 fusion.21
  9.9 1.7 collective-permute-start
  11.6 7.4 %collective-permute-start.1 = (bf16[1,4,24,512]{3,2,1,0:T(8,128)(2,1)}, bf16[1,4,24,512]{3,2,1,0:T(8,128)(2,1)}, u32[]{:S(2)}, u32[]{:S(2)}) collective-permute-start(bf16[1,4,24,512]{3,2,1,0:T(8,128)(2,1)} %get-tuple-element.15), channel_id=1, source_target_pairs={{4,0},{8,4},{12,8},{16,12},{20,16},{24,20},{28,24},{32,28},{36,32}... | collective-permute-start | bytes 294920 | tf_op jit(solution)/shard_map/ppermute | solution.py:26
  19.4 2.1 reshape.270
  21.5 0.7 reshape.268
  22.2 0.8 bitcast_convert_fusion.2
  23.0 0.8 bitcast_convert_fusion.1
  23.9 1.0 pad_maximum_fusion.3
  24.9 1.7 collective-permute-start.3
  26.8 3.3 add.265
  30.0 6.5 %add.266 = f32[144,6144]{1,0:T(8,128)} reshape(f32[2,8,3,3,6144]{4,3,2,1,0:T(4,128)} %add.265) | data formatting | bytes 7077888 | tf_op jit(solution)/shard_map/add | solution.py:55
  36.5 3.3 add.271
  39.7 6.4 %add.272 = f32[144,6144]{1,0:T(8,128)} reshape(f32[2,8,3,3,6144]{4,3,2,1,0:T(4,128)} %add.271) | data formatting | bytes 7077888 | tf_op jit(solution)/shard_map/add | solution.py:56
  46.1 3.3 add.260
  49.4 6.4 %add.261 = f32[144,6144]{1,0:T(8,128)} reshape(f32[2,8,3,3,6144]{4,3,2,1,0:T(4,128)} %add.260) | data formatting | bytes 7077888 | tf_op jit(solution)/shard_map/add | solution.py:54
  55.9 3.0 maximum_select_fusion
  58.9 2.0 fusion.29
  60.9 1.9 fusion.31
  62.7 0.8 fusion.33
  63.5 0.8 fusion.35
  64.4 0.8 fusion.37
  65.2 0.9 fusion.39
  66.0 0.8 fusion.41
  66.9 0.8 fusion.43
  68.1 1.6 fusion.17
  70.4 1.5 copy.53
  71.9 7.6 %all-to-all-start = ((bf16[32,6,1,6,512]{4,3,1,2,0:T(8,128)(2,1)}), bf16[32,6,1,6,512]{4,3,1,2,0:T(8,128)(2,1)S(1)}, u32[]{:S(2)}, u32[]{:S(2)}) async-start(bf16[32,6,1,6,512]{4,3,1,2,0:T(8,128)(2,1)} %bitcast.163), calls=%async_computation | async-start | bytes 3145728 | tf_op jit(solution)/shard_map/all_to_all | solution.py:120
  80.2 23.2 %all-to-all-done = bf16[32,6,1,6,512]{4,3,1,2,0:T(8,128)(2,1)S(1)} async-done(((bf16[32,6,1,6,512]{4,3,1,2,0:T(8,128)(2,1)}), bf16[32,6,1,6,512]{4,3,1,2,0:T(8,128)(2,1)S(1)}, u32[]{:S(2)}, u32[]{:S(2)}) %all-to-all-start) | async-done | bytes 1179680 | tf_op jit(solution)/shard_map/all_to_all | solution.py:120
  103.4 0.8 fusion.93
  104.2 0.7 copy-done.4
  105.3 1.1 convolution_add_fusion.3
  106.4 1.5 fusion.50
  109.8 1.4 convolution_add_fusion.2
  111.2 1.5 fusion.49
  113.2 5.2 %fusion.95 = (f32[144]{0:T(256)S(1)}, f32[144,6144]{1,0:T(8,128)S(1)}) fusion(f32[144,6144]{1,0:T(8,128)} %add.272, f32[144,6144]{1,0:T(8,128)} %add.266, f32[144,6144]{1,0:T(8,128)} %add.261, f32[6144]{0:T(1024)S(1)} %copy-done.14, bf16[144,64]{1,0:T(8,128)(2,1)S(1)} %convert_element_type.70, bf16[64,6144]{1,0:T(8,128)(2,1)S(1)} %copy-done), kind=kOutput, calls=%fused_computation.123 | convolution fusion | flops 117669744 | bytes 14985792 | tf_op jit(solution)/shard_map/dot_general | solution.py:44
  119.1 1.9 add_convert_fusion
  121.1 0.7 all-gather.5.cloned.1.call-update
  121.9 67.1 %all-gather.3.cloned.1.call-done = bf16[576,6144]{1,0:T(8,128)(2,1)} async-done(((bf16[144,6144]{1,0:T(8,128)(2,1)}), bf16[576,6144]{1,0:T(8,128)(2,1)}) %all-gather.3.cloned.1.call-update) | async-done | bytes 7077904 | tf_op jit(solution)/shard_map/all_gather | solution.py:157
  189.0 234.5 %all-gather.5.cloned.1.call-done = bf16[3,6144,768]{2,1,0:T(8,128)(2,1)} async-done(((bf16[3,192,768]{2,1,0:T(8,128)(2,1)}), bf16[3,6144,768]{2,1,0:T(8,128)(2,1)}) %all-gather.5.cloned.1.call-update) | async-done | bytes 28311568 | tf_op jit(solution)/shard_map/all_gather | solution.py:161
  423.5 21.5 %fusion.5 = f32[3,576,768]{2,1,0:T(8,128)S(1)} fusion(bf16[3,6144,768]{2,1,0:T(8,128)(2,1)} %all-gather.5.cloned.1.call-done, bf16[576,6144]{1,0:T(8,128)(2,1)} %all-gather.3.cloned.1.call-done), kind=kOutput, calls=%fused_computation.11 | convolution fusion | flops 16307453952 | bytes 40697856 | tf_op jit(solution)/shard_map/tr,krh->kth/dot_general | solution.py:158
  445.0 2.2 slice_multiply_fusion
  447.2 1.4 copy-done.2
  448.5 1.0 fusion.51
  449.5 1.9 copy.36
  451.6 1.8 copy.37
  453.5 1.9 copy.38
  455.6 1.8 copy.39
  457.4 4.8 %fusion.23 = (bf16[576,768]{1,0:T(8,128)(2,1)}, bf16[576,768]{1,0:T(8,128)(2,1)}) fusion(f32[576,768]{1,0:T(8,128)} %copy.39, f32[3,576,768]{2,1,0:T(8,128)} %copy-done.2, f32[768]{0:T(1024)S(1)} %get-tuple-element.3, f32[768]{0:T(1024)S(1)} %get-tuple-element.4, f32[576,768]{1,0:T(8,128)} %copy.37), kind=kLoop, calls=%fused_computation.30 | loop fusion | flops 2654208 | bytes 8853504 | tf_op jit(solution)/shard_map/convert_element_type | solution.py:37
  (76 shorter events, 7.0 us)
Async XLA Ops:
  7.2 106.0 %copy-start = (bf16[64,6144]{1,0:T(8,128)(2,1)S(1)}, bf16[64,6144]{1,0:T(8,128)(2,1)}, u32[]{:S(2)}) copy-start(bf16[64,6144]{1,0:T(8,128)(2,1)} %param.22) | copy-start | bytes 2359300
  7.2 11.8 %copy-start.7 = (bf16[48,6144]{1,0:T(8,128)(2,1)S(1)}, bf16[48,6144]{1,0:T(8,128)(2,1)}, u32[]{:S(2)}) copy-start(bf16[48,6144]{1,0:T(8,128)(2,1)} %param.25) | copy-start | bytes 1769476
  7.2 14.3 %copy-start.11 = (bf16[8,6144]{1,0:T(8,128)(2,1)S(1)}, bf16[8,6144]{1,0:T(8,128)(2,1)}, u32[]{:S(2)}) copy-start(bf16[8,6144]{1,0:T(8,128)(2,1)} %param.24) | copy-start | bytes 294916
  9.9 13.9 %collective-permute-start = (bf16[1,4,24,512]{3,2,1,0:T(8,128)(2,1)}, bf16[1,4,24,512]{3,2,1,0:T(8,128)(2,1)}, u32[]{:S(2)}, u32[]{:S(2)}) collective-permute-start(bf16[1,4,24,512]{3,2,1,0:T(8,128)(2,1)} %get-tuple-element.14), channel_id=1, source_target_pairs={{0,4},{4,8},{8,12},{12,16},{16,20},{20,24},{24,28},{28,32},{32,36}... | collective-permute-start | bytes 294920 | tf_op jit(solution)/shard_map/ppermute | solution.py:24
  11.6 12.3 %collective-permute-start.1 = (bf16[1,4,24,512]{3,2,1,0:T(8,128)(2,1)}, bf16[1,4,24,512]{3,2,1,0:T(8,128)(2,1)}, u32[]{:S(2)}, u32[]{:S(2)}) collective-permute-start(bf16[1,4,24,512]{3,2,1,0:T(8,128)(2,1)} %get-tuple-element.15), channel_id=1, source_target_pairs={{4,0},{8,4},{12,8},{16,12},{20,16},{24,20},{28,24},{32,28},{36,32}... | collective-permute-start | bytes 294920 | tf_op jit(solution)/shard_map/ppermute | solution.py:26
  24.9 31.0 %collective-permute-start.2 = (bf16[14,4,1,512]{3,2,1,0:T(2,128)(2,1)S(1)}, bf16[14,4,1,512]{3,2,1,0:T(2,128)(2,1)S(1)}, u32[]{:S(2)}, u32[]{:S(2)}) collective-permute-start(bf16[14,4,1,512]{3,2,1,0:T(2,128)(2,1)S(1)} %get-tuple-element.12), channel_id=1, source_target_pairs={{0,1},{1,2},{2,3},{3,0},{4,5},{5,6},{6,7},{7,4},{8,9},{9,10},{10,1... | collective-permute-start | bytes 172040 | tf_op jit(solution)/shard_map/ppermute | solution.py:24
  24.9 30.9 %collective-permute-start.3 = (bf16[14,4,1,512]{3,2,1,0:T(2,128)(2,1)S(1)}, bf16[14,4,1,512]{3,2,1,0:T(2,128)(2,1)S(1)}, u32[]{:S(2)}, u32[]{:S(2)}) collective-permute-start(bf16[14,4,1,512]{3,2,1,0:T(2,128)(2,1)S(1)} %get-tuple-element.13), channel_id=1, source_target_pairs={{1,0},{2,1},{3,2},{0,3},{5,4},{6,5},{7,6},{4,7},{9,8},{10,9},{11,1... | collective-permute-start | bytes 172040 | tf_op jit(solution)/shard_map/ppermute | solution.py:26
  55.9 6.9 %slice-start = ((s8[4718592]{0:T(1024)(128)(4,1)}), s8[524288]{0:T(1024)(128)(4,1)S(1)}, s32[]{:S(2)}) async-start(s8[4718592]{0:T(1024)(128)(4,1)} %bitcast.165), calls=%async_computation.3 | async-start | bytes 1048576
  58.9 3.9 slice-start.1
  66.8 1.3 copy-start.3
  66.8 1.3 copy-start.17
  70.4 9.2 %copy-start.13 = (f32[2,6144]{1,0:T(2,128)S(1)}, f32[2,6144]{1,0:T(2,128)}, u32[]{:S(2)}) copy-start(f32[2,6144]{1,0:T(2,128)} %param.27) | copy-start | bytes 147460
  71.9 32.3 %copy-start.15 = (f32[512]{0:T(512)S(1)}, f32[512]{0:T(512)}, u32[]{:S(2)}) copy-start(f32[512]{0:T(512)} %param.19) | copy-start | bytes 6148
  71.9 31.5 %all-to-all-start = ((bf16[32,6,1,6,512]{4,3,1,2,0:T(8,128)(2,1)}), bf16[32,6,1,6,512]{4,3,1,2,0:T(8,128)(2,1)S(1)}, u32[]{:S(2)}, u32[]{:S(2)}) async-start(bf16[32,6,1,6,512]{4,3,1,2,0:T(8,128)(2,1)} %bitcast.163), calls=%async_computation | async-start | bytes 3145728 | tf_op jit(solution)/shard_map/all_to_all | solution.py:120
  79.5 109.5 %all-gather.3.cloned.1.call-start = ((), (), s32[]{:S(2)}) async-start(), calls=%async_computation.1 | async-start | bytes 8847360 | tf_op jit(solution)/shard_map/all_gather | solution.py:157
  80.2 26.2 %copy-start.12 = (bf16[512,16]{0,1:T(8,128)(2,1)S(1)}, bf16[512,16]{0,1:T(8,128)(2,1)}, u32[]{:S(2)}) copy-start(bf16[512,16]{0,1:T(8,128)(2,1)} %param.20) | copy-start | bytes 49156
  80.2 26.2 %copy-start.18 = (f32[16]{0:T(128)S(1)}, f32[16]{0:T(128)}, u32[]{:S(2)}) copy-start(f32[16]{0:T(128)} %param.21) | copy-start | bytes 196
  103.4 1.6 copy-start.4
  108.6 1.1 copy-start.5
  108.6 1.2 copy-start.6
  109.5 3.3 copy-start.8
  109.8 3.4 copy-start.14
  118.4 0.7 copy-start.9
  118.4 0.8 copy-start.10
  121.0 0.8 copy-start.16
  121.1 302.4 %all-gather.5.cloned.1.call-start = ((), (), s32[]{:S(2)}) async-start(), calls=%async_computation.2 | async-start | bytes 29196288 | tf_op jit(solution)/shard_map/all_gather | solution.py:161
  445.0 3.5 copy-start.2
  457.4 4.8 %copy-start.1 = (bf16[64,6144]{1,0:T(8,128)(2,1)S(1)}, bf16[64,6144]{1,0:T(8,128)(2,1)}, u32[]{:S(2)}) copy-start(bf16[64,6144]{1,0:T(8,128)(2,1)} %param.22) | copy-start | bytes 2359300
Sparse Core Ops, SparseCore 0:
  121.2 67.7 all-gather.2
  192.0 231.4 all-gather.4
where the time goes:
time: 471 us; the launch traced here: 469 us
  waiting for transfers between devices  326 us (69%)
  local copies, waits for them, and re-layouts  49.3 us (10%)
  matrix products  42.9 us (9%)
  starting transfers between devices  18.5 us (4%)
  other arithmetic  18.3 us (4%)
  between operations  14.5 us (3%)
    all_gather x1, waiting for transfers between devices, body(): lax.all_gather(qkv_weight, 'fsdp', axis=1, tiled=True)  235 us
    all_gather x1, waiting for transfers between devices, body(): normed = lax.all_gather(local_rows, 'cp', axis=0, tiled=True)  67.1 us
    all_to_all x1, waiting for transfers between devices, body(): lax.all_to_all(outgoing, 'fsdp', split_axis=0, concat_axis=0, tiled=True)  23.2 us
    dot_general x1, matrix products, body(): jnp.einsum('tr,krh->kth', normed, lax.all_gather(qkv_weight, 'fsdp', axis...  21.5 us
    dot_general x9, matrix products, body(): jnp.dot(region, conv_weight[row_shift, col_shift], preferred_element_type...  10.4 us
    add x2, local copies, waits for them, and re-layouts, embed_tokens(): grid = grid + row_table.astype(jnp.float32)[None, None, None, :, :, None, :]  9.73 us
    add x2, local copies, waits for them, and re-layouts, embed_tokens(): grid + window_table.astype(jnp.float32)[None, :, :, None, None, None, :]  9.7 us
    add x2, local copies, waits for them, and re-layouts, embed_tokens(): grid = grid + col_table.astype(jnp.float32)[:, None, None, None, None, :, :]  9.66 us
  transfers between devices with their start and end apart: 7, of which 3 were waited for; matrix products, arithmetic and copies ran while one was open for 7% of the time, Pallas kernels for 0%

commit v1 on v0

v1 whole, which is shorter than its diff:
```python
import jax
import jax.numpy as jnp
from jax import lax
from jax.sharding import PartitionSpec as P

D = 6144
HD = 128
C = 512
LAT = 16
FR = 4
H = 96
ROW_SPLIT = 2
COL_SPLIT = 4
HIGHEST = lax.Precision.HIGHEST


def padded_2(cells, sides, width):
    for axis, dim in sides:
        count = lax.axis_size(axis)
        head = lax.slice_in_dim(cells, 0, width, axis=dim)
        tail = lax.slice_in_dim(cells, cells.shape[dim] - width, cells.shape[dim], axis=dim)
        cells = jnp.concatenate(
            [
                lax.ppermute(tail, axis, [(i, (i + 1) % count) for i in range(count)]),
                cells,
                lax.ppermute(head, axis, [((i + 1) % count, i) for i in range(count)]),
            ],
            axis=dim,
        )
    return cells


def head_norm(projected_part, gain_row):
    count = projected_part.shape[0]
    shaped = projected_part.reshape(count, -1, HD)
    scale = lax.rsqrt(jnp.mean(shaped * shaped, axis=-1, keepdims=True) + 1e-06)
    return ((shaped * scale).reshape(count, -1) * gain_row).astype(jnp.bfloat16)


def halves(values):
    high = values.astype(jnp.bfloat16)
    low = (values - high.astype(jnp.float32)).astype(jnp.bfloat16)
    return high, low


def body(
    video,
    conv_weight,
    conv_bias,
    time_weight,
    time_bias,
    latent_weight,
    latent_bias,
    patch_weight,
    patch_bias,
    frame_pos,
    row_pos,
    col_pos,
    modulation,
    qkv_weight,
    qk_gain,
):
    f32 = jnp.float32
    fsdp_count = lax.axis_size("fsdp")
    cp_count = lax.axis_size("cp")
    position = lax.axis_index("fsdp")
    column = lax.axis_index("cp")
    block_rows = video.shape[0]
    window_count = video.shape[1]
    col_block = video.shape[2]
    row_blocks = H // block_rows
    half_blocks = row_blocks // 2
    block_index = (position + row_blocks - half_blocks) % row_blocks
    frame = ((position + fsdp_count - half_blocks) % fsdp_count) // row_blocks
    tables = jnp.concatenate(
        [
            patch_weight.astype(f32),
            frame_pos.astype(f32) + patch_bias,
            row_pos.astype(f32),
            col_pos.astype(f32),
        ],
        axis=0,
    )
    centered = (tables - jnp.mean(tables, axis=1, keepdims=True)) * (1.0 + modulation[0])
    centered = jnp.concatenate([centered, modulation[1:2]], axis=0)
    own_rows = qkv_weight.shape[1]
    own = lax.dynamic_slice_in_dim(centered, position * own_rows, own_rows, 1)
    own_high, own_low = halves(own)
    parts = jnp.einsum(
        "tr,krh->tkh",
        jnp.concatenate([own_high, own_low], axis=0),
        qkv_weight,
        preferred_element_type=f32,
    )
    count = own.shape[0]
    panel = lax.psum(parts[:count] + parts[count:], "fsdp")
    folded = jnp.einsum(
        "jco,ol->jcl", time_weight, latent_weight, preferred_element_type=f32
    )
    zeros = jnp.zeros_like(folded[0])
    early = jnp.stack([folded[1], folded[2], zeros, zeros])
    late = jnp.stack([zeros, folded[0], folded[1], folded[2]])
    both = jnp.concatenate(
        [
            lax.dynamic_index_in_dim(early, frame, 0, False),
            lax.dynamic_index_in_dim(late, frame, 0, False),
        ],
        axis=1,
    )
    high, low = halves(both)
    wide = jnp.concatenate([high, low], axis=1)
    kernel = jnp.einsum("abco,ol->abcl", conv_weight, wide, preferred_element_type=f32)
    kernel = kernel[..., : 2 * LAT] + kernel[..., 2 * LAT :]
    kernel_high, kernel_low = halves(kernel)
    active = jax.nn.silu(video.astype(f32)).astype(jnp.bfloat16)
    padded = padded_2(active, (("fsdp", 0), ("cp", 2)), 1)
    row_ids = lax.broadcasted_iota(jnp.int32, (block_rows + 2, 1, 1, 1), 0)
    col_ids = lax.broadcasted_iota(jnp.int32, (1, 1, col_block + 2, 1), 2)
    dropped_rows = (row_ids == 0) & (block_index == 0) | (row_ids == block_rows + 1) & (
        block_index == row_blocks - 1
    )
    dropped_cols = (col_ids == 0) & (column == 0) | (col_ids == col_block + 1) & (
        column == cp_count - 1
    )
    padded = jnp.where(dropped_rows | dropped_cols, jnp.zeros((), jnp.bfloat16), padded)
    kernels = jnp.concatenate([kernel_high, kernel_low], axis=-1)
    kernels = kernels.transpose(2, 0, 1, 3).reshape(C, -1)
    through = jnp.dot(padded, kernels, preferred_element_type=f32)
    through = through.reshape(*padded.shape[:3], 3, 3, 2, 2 * LAT).sum(axis=5)
    direct = jnp.dot(video, wide, preferred_element_type=f32)
    running = direct[..., : 2 * LAT] + direct[..., 2 * LAT :]
    running = running + jnp.dot(conv_bias, both, precision=HIGHEST)
    for row_shift in range(3):
        for col_shift in range(3):
            running = running + through[
                row_shift : row_shift + block_rows,
                :,
                col_shift : col_shift + col_block,
                row_shift,
                col_shift,
            ]
    sub_rows = block_rows // ROW_SPLIT
    sub_cols = col_block // COL_SPLIT
    outgoing = running.reshape(ROW_SPLIT, sub_rows, window_count, COL_SPLIT, sub_cols, 2 * LAT)
    outgoing = outgoing.transpose(2, 0, 3, 1, 4, 5).reshape(fsdp_count, -1)
    tiles = lax.all_to_all(outgoing, "fsdp", split_axis=0, concat_axis=0, tiled=True)
    tiles = jnp.roll(tiles, -half_blocks, axis=0)
    half_rows = sub_rows // 2
    half_cols = sub_cols // 2
    tiles = tiles.reshape(FR, row_blocks, half_rows, 2, half_cols, 2, 2, LAT).sum(axis=0)
    offset = jnp.dot(time_bias, latent_weight.astype(f32), precision=HIGHEST) + latent_bias
    tiles = tiles + offset
    patches = tiles.transpose(5, 0, 1, 3, 2, 4, 6).reshape(-1, 4 * LAT).astype(jnp.bfloat16)
    row_part = position // COL_SPLIT % ROW_SPLIT
    col_part = position % COL_SPLIT
    group_index = position // (ROW_SPLIT * COL_SPLIT)

    def select(frames, rows, cols):
        width = frames.shape[-1]
        frames = lax.dynamic_slice_in_dim(frames, group_index * 2, 2, 0)
        rows = lax.dynamic_index_in_dim(
            rows.reshape(row_blocks, ROW_SPLIT, half_rows, width), row_part, 1, False
        )
        cols = lax.dynamic_index_in_dim(
            cols.reshape(cp_count, COL_SPLIT, half_cols, width), col_part, 1, False
        )
        return frames, rows, cols

    def embed(values, weight, frames, rows, cols):
        base = jnp.dot(values, weight, preferred_element_type=f32, precision=HIGHEST)
        shaped = base.reshape(cols.shape[0], 2, row_blocks, half_rows, half_cols, -1)
        shaped = shaped + frames[None, :, None, None, None, :]
        shaped = shaped + rows[None, None, :, :, None, :]
        shaped = shaped + cols[:, None, None, None, :, :]
        return shaped.reshape(base.shape)

    frames, rows, cols = select(frame_pos.astype(f32) + patch_bias, row_pos, col_pos)
    own_cols = lax.dynamic_slice_in_dim(cols, column, 1, 0)
    embedded = embed(patches, patch_weight, frames, rows.astype(f32), own_cols.astype(f32))
    center = jnp.mean(embedded, axis=-1, keepdims=True)
    spread = jnp.mean((embedded - center) ** 2, axis=-1, keepdims=True)
    scale = lax.rsqrt(spread + 1e-06)
    packed = jnp.concatenate([patches.astype(f32), scale], axis=1)
    packed = lax.all_gather(packed, "cp", axis=0, tiled=True)
    panel = panel.reshape(count, -1)
    heads = qkv_weight.shape[2]
    frames, rows, cols = select(panel[64:72], panel[72:120], panel[120:168])
    projected = embed(packed[:, :64], panel[:64], frames, rows, cols)
    projected = projected * packed[:, 64:65] + panel[168]
    query = head_norm(projected[:, :heads], qk_gain[0])
    keys = head_norm(projected[:, heads : 2 * heads], qk_gain[1])
    values = projected[:, 2 * heads :].astype(jnp.bfloat16)
    return (query, keys, values)


def solution(mesh):
    return jax.shard_map(
        body,
        mesh=mesh,
        in_specs=(
            P("fsdp", None, "cp", None),
            P(),
            P(),
            P(),
            P(),
            P(),
            P(),
            P(),
            P(),
            P(),
            P(),
            P(),
            P(),
            P(None, "fsdp", "cp"),
            P(None, "cp"),
        ),
        out_specs=(P("fsdp", "cp"), P("fsdp", "cp"), P("fsdp", "cp")),
        check_vma=False,
    )
```

time: 471 us -> 426 us (0.904)
  waiting for transfers between devices: 326 us -> 302 us
  matrix products: 42.9 us -> 19.5 us
  local copies, waits for them, and re-layouts: 49.3 us -> 41.2 us
  other arithmetic: 18.3 us -> 24.6 us
  blocking collectives: 0 us -> 6.28 us
    all_gather x2 -> x0, waiting for transfers between devices: 302 us -> none  [the longest x1 235 us: body(): lax.all_gather(qkv_weight, 'fsdp', axis=1, tiled=True)]
    psum x0 -> x1, waiting for transfers between devices: none -> 289 us  [body(): panel = lax.psum(parts[:count] + parts[count:], 'fsdp')]
    dot_general x16 -> x9, matrix products: 42.9 us -> 19.5 us  [the longest x1 8.35 us: body(): through = jnp.dot(padded, kernels, preferred_element_type=f32)]
    add x6 -> x4, local copies, waits for them, and re-layouts: 29.1 us -> 5.85 us  [the longest x2 5.69 us: embed(): shaped = shaped + cols[:, None, None, None, :, :]]
    all_to_all x1, waiting for transfers between devices: 23.2 us -> 9.81 us  [body(): lax.all_to_all(outgoing, 'fsdp', split_axis=0, concat_axis=0, tiled=True)]
    reshape x4 -> x6, local copies, waits for them, and re-layouts: 4.7 us -> 14.3 us  [the longest x1 8.72 us: embed(): return shaped.reshape(base.shape)]
    all_gather x0 -> x1, blocking collectives: none -> 6.28 us  [body(): packed = lax.all_gather(packed, 'cp', axis=0, tiled=True)]
    slice x2 -> x13, local copies, waits for them, and re-layouts: 0.87 us -> 6.03 us  [the longest x4 2.72 us: body(): frames, rows, cols = select(panel[64:72], panel[72:120], panel[120:168])]
  transfers between devices with their start and end apart: 7 -> 6, of which waited for: 3 -> 3; matrix products, arithmetic and copies ran while one was open for 7% -> 8% of each run, Pallas kernels for 0% -> 0%
where the time goes in v1:
time: 426 us; the launch traced here: 424 us
  waiting for transfers between devices  302 us (71%)
  local copies, waits for them, and re-layouts  41.2 us (10%)
  other arithmetic  24.6 us (6%)
  matrix products  19.5 us (5%)
  starting transfers between devices  15.4 us (4%)
  between operations  14.9 us (3%)
  blocking collectives  6.28 us (1%)
    psum x1, waiting for transfers between devices, body(): panel = lax.psum(parts[:count] + parts[count:], 'fsdp')  289 us
    all_to_all x1, waiting for transfers between devices, body(): lax.all_to_all(outgoing, 'fsdp', split_axis=0, concat_axis=0, tiled=True)  9.81 us
    ppermute x2, starting transfers between devices, padded_2(): lax.ppermute(head, axis, [((i + 1) % count, i) for i in range(count)])  9.11 us
    reshape x1, local copies, waits for them, and re-layouts, embed(): return shaped.reshape(base.shape)  8.72 us
  transfers between devices with their start and end apart: 6, of which 3 were waited for; matrix products, arithmetic and copies ran while one was open for 8% of the time, Pallas kernels for 0%

profile of v1, /device:TPU:0, one launch (start us, length us, event | category | flops | bytes accessed | tf_op | source)
XLA Modules:
  0.0 424.1 jit_solution(262450259091125447)
XLA Ops:
  7.3 2.1 fusion.6
  9.4 1.0 copy-done.5
  10.4 0.7 fusion.53
  11.1 1.7 collective-permute-start
  12.7 7.4 %collective-permute-start.1 = (bf16[1,4,24,512]{3,2,1,0:T(8,128)(2,1)}, bf16[1,4,24,512]{3,2,1,0:T(8,128)(2,1)}, u32[]{:S(2)}, u32[]{:S(2)}) collective-permute-start(bf16[1,4,24,512]{3,2,1,0:T(8,128)(2,1)} %get-tuple-element.18), channel_id=1, source_target_pairs={{4,0},{8,4},{12,8},{16,12},{20,16},{24,20},{28,24},{32,28},{36,32}... | collective-permute-start | bytes 294920 | tf_op jit(solution)/shard_map/ppermute | solution.py:26
  20.4 1.9 convert_element_type.113
  22.7 2.3 subtract_multiply_fusion
  25.2 1.0 copy-done.12
  26.2 0.6 fusion.36
  26.8 1.3 slice_add_fusion
  28.3 0.5 fusion.43
  28.8 0.7 copy-done.13
  29.5 0.8 fusion.41
  30.3 1.1 reshape.232
  31.4 2.1 reshape.233
  33.5 0.6 constant_dynamic-slice_fusion.2
  34.1 0.5 convolution_bitcast_fusion.1
  34.6 3.9 convolution_bitcast_fusion
  38.7 1.2 bitcast_convert_fusion
  39.9 0.8 bitcast_convert_fusion.1
  40.8 1.0 pad_maximum_fusion.5
  41.9 1.7 collective-permute-start.3
  43.7 3.2 collective-permute-done.2
  46.9 8.3 %convolution_reduce_fusion = f32[14,4,26,3,3,32]{5,2,4,3,1,0:T(8,128)S(1)} fusion(bf16[3,3,2,32,512,1,1]{4,3,2,1,0,6,5:T(8,128)(2,1)S(1)} %bitcast.172, bf16[14,4,1,512]{3,2,1,0:T(2,128)(2,1)S(1)} %collective-permute-done.3, bf16[1,4,24,512]{3,2,1,0:T(8,128)(2,1)} %collective-permute-done.1, bf16[12,4,24,512]{3,2,1,0:T(8,128)(2,1)S(1)} %copy-done.6, ...), kind=kOutput, calls=%fused_computation.7 | convolution fusion | flops 867403264 | bytes 3758444 | tf_op jit(solution)/shard_map/dot_general | solution.py:128
  55.3 0.8 fusion.21
  56.4 1.0 all_to_all.8
  57.4 4.5 %all-to-all-start = ((f32[32,1,1152]{2,1,0:T(1,128)}), f32[32,1,1152]{2,1,0:T(1,128)S(1)}, u32[]{:S(2)}, u32[]{:S(2)}) async-start(f32[32,1,1152]{2,1,0:T(1,128)} %all_to_all.8), calls=%async_computation | async-start | bytes 294912 | tf_op jit(solution)/shard_map/all_to_all | solution.py:146
  62.4 9.8 %all-to-all-done = f32[32,1,1152]{2,1,0:T(1,128)S(1)} async-done(((f32[32,1,1152]{2,1,0:T(1,128)}), f32[32,1,1152]{2,1,0:T(1,128)S(1)}, u32[]{:S(2)}, u32[]{:S(2)}) %all-to-all-start) | async-done | bytes 147488 | tf_op jit(solution)/shard_map/all_to_all | solution.py:146
  72.4 1.5 reshape.231
  73.9 0.9 reduce_sum.64
  75.5 0.8 fusion.55
  76.3 0.5 multiply_reduce_fusion
  77.1 6.3 %all_gather.3 = f32[576,65]{1,0:T(8,128)S(1)} all-gather(f32[144,65]{1,0:T(8,128)S(1)} %pad_maximum_fusion.6), channel_id=1, replica_groups=mesh['fsdp'=32,'cp'=4] {'cp'}, dimensions={0}, use_global_device_ids=true | all-gather | bytes 187200 | tf_op jit(solution)/shard_map/all_gather | solution.py:184
  83.8 289.2 %all-reduce.4.cloned.1.call-done = f32[169,3,768]{2,0,1:T(8,128)} async-done(((f32[169,3,768]{2,0,1:T(8,128)}), f32[169,3,768]{2,0,1:T(8,128)}) %all-reduce.4.cloned.1.call-update) | async-done | bytes 1557520 | tf_op jit(solution)/shard_map/psum | solution.py:96
  373.0 0.9 slice_reduce_fusion.1
  374.0 0.9 slice.194
  374.9 1.2 fusion.52
  378.7 4.7 %add_add_fusion = f32[4,2,8,3,3,2304]{5,2,4,3,1,0:T(8,128)S(1)} fusion(f32[4,3,2304]{2,1,0:T(4,128)S(1)} %dynamic-slice_bitcast_fusion, f32[8,3,2304]{2,0,1:T(8,128)S(1)} %bitcast.168, f32[2,2304]{1,0:T(2,128)S(1)} %constant_dynamic-slice_fusion.1, f32[64,2304,1,1,1,1]{1,0,2,3,4,5:T(8,128)S(1)} %reshape.250, f32[4,2,8,3,3,64]{5,4,3,2,1,0:T(4,128)S(1)} %dot_general.48), kind=kOutput, calls=%fused_computation.4 | convolution fusion | flops 1023197184 | bytes 6395904 | tf_op jit(solution)/shard_map/dot_general | solution.py:170
  383.4 5.7 %copy.125 = f32[4,2,8,3,3,2304]{5,4,3,2,1,0:T(4,128)} copy(f32[4,2,8,3,3,2304]{5,2,4,3,1,0:T(8,128)S(1)} %add_add_fusion) | data formatting | bytes 10616832 | tf_op jit(solution)/shard_map/add | solution.py:174
  389.1 8.7 %reshape.236 = f32[576,2304]{1,0:T(8,128)} reshape(f32[4,2,8,3,3,2304]{5,4,3,2,1,0:T(4,128)} %copy.125) | data formatting | bytes 10616832 | tf_op jit(solution)/shard_map/reshape | solution.py:175
  397.8 3.0 multiply_add_fusion
  400.8 1.1 slice.273
  401.9 2.5 slice_multiply_fusion
  404.5 1.9 copy.128
  406.6 1.8 copy.129
  408.4 1.9 copy.126
  410.5 1.8 copy.127
  412.3 4.9 %multiply_convert_fusion = (bf16[576,768]{1,0:T(8,128)(2,1)}, bf16[576,768]{1,0:T(8,128)(2,1)}) fusion(f32[576,768]{1,0:T(8,128)} %copy.129, f32[576,2304]{1,0:T(8,128)} %copy-done.2, f32[768]{0:T(1024)S(1)} %get-tuple-element.3, f32[768]{0:T(1024)S(1)} %get-tuple-element.4, f32[576,768]{1,0:T(8,128)} %copy.127), kind=kLoop, calls=%fused_computation.30 | loop fusion | flops 2654208 | bytes 8853504 | tf_op jit(solution)/shard_map/convert_element_type | solution.py:37
  (106 shorter events, 6.8 us)
Async XLA Ops:
  7.2 21.1 %copy-start = (bf16[3,512,512]{2,1,0:T(8,128)(2,1)S(1)}, bf16[3,512,512]{2,1,0:T(8,128)(2,1)}, u32[]{:S(2)}) copy-start(bf16[3,512,512]{2,1,0:T(8,128)(2,1)} %param.18) | copy-start | bytes 4718596
  7.2 12.9 %copy-start.16 = (f32[2,6144]{1,0:T(2,128)S(1)}, f32[2,6144]{1,0:T(2,128)}, u32[]{:S(2)}) copy-start(f32[2,6144]{1,0:T(2,128)} %param.27) | copy-start | bytes 147460
  7.2 13.0 %copy-start.9 = (bf16[48,6144]{1,0:T(8,128)(2,1)S(1)}, bf16[48,6144]{1,0:T(8,128)(2,1)}, u32[]{:S(2)}) copy-start(bf16[48,6144]{1,0:T(8,128)(2,1)} %param.25) | copy-start | bytes 1769476
  7.2 13.0 %copy-start.11 = (bf16[48,6144]{1,0:T(8,128)(2,1)S(1)}, bf16[48,6144]{1,0:T(8,128)(2,1)}, u32[]{:S(2)}) copy-start(bf16[48,6144]{1,0:T(8,128)(2,1)} %param.26) | copy-start | bytes 1769476
  7.2 365.8 %all-reduce.4.cloned.1.call-start = ((), (), s32[]{:S(2)}) async-start(), calls=%async_computation.1 | async-start | bytes 3244032 | tf_op jit(solution)/shard_map/psum | solution.py:96
  9.4 1.0 copy-start.5
  11.1 29.7 %collective-permute-start = (bf16[1,4,24,512]{3,2,1,0:T(8,128)(2,1)}, bf16[1,4,24,512]{3,2,1,0:T(8,128)(2,1)}, u32[]{:S(2)}, u32[]{:S(2)}) collective-permute-start(bf16[1,4,24,512]{3,2,1,0:T(8,128)(2,1)} %get-tuple-element.17), channel_id=1, source_target_pairs={{0,4},{4,8},{8,12},{12,16},{16,20},{20,24},{24,28},{28,32},{32,36}... | collective-permute-start | bytes 294920 | tf_op jit(solution)/shard_map/ppermute | solution.py:24
  12.7 28.0 %collective-permute-start.1 = (bf16[1,4,24,512]{3,2,1,0:T(8,128)(2,1)}, bf16[1,4,24,512]{3,2,1,0:T(8,128)(2,1)}, u32[]{:S(2)}, u32[]{:S(2)}) collective-permute-start(bf16[1,4,24,512]{3,2,1,0:T(8,128)(2,1)} %get-tuple-element.18), channel_id=1, source_target_pairs={{4,0},{8,4},{12,8},{16,12},{20,16},{24,20},{28,24},{32,28},{36,32}... | collective-permute-start | bytes 294920 | tf_op jit(solution)/shard_map/ppermute | solution.py:26
  20.2 2.5 copy-start.3
  20.3 2.0 copy-start.15
  20.3 2.0 copy-start.17
  20.4 2.3 copy-start.4
  25.0 1.2 copy-start.12
  26.8 1.5 copy-start.18
  28.1 2.1 copy-start.10
  28.3 5.8 %copy-start.7 = (bf16[12,4,24,512]{3,2,1,0:T(8,128)(2,1)S(1)}, bf16[12,4,24,512]{3,2,1,0:T(8,128)(2,1)}, u32[]{:S(2)}) copy-start(bf16[12,4,24,512]{3,2,1,0:T(8,128)(2,1)} %param.15) | copy-start | bytes 3538948
  28.8 0.7 copy-start.13
  38.4 2.3 copy-start.6
  38.6 5.0 %copy-start.20 = (f32[512]{0:T(512)S(1)}, f32[512]{0:T(512)}, u32[]{:S(2)}) copy-start(f32[512]{0:T(512)} %param.17) | copy-start | bytes 6148
  41.8 5.2 %collective-permute-start.2 = (bf16[14,4,1,512]{3,2,1,0:T(2,128)(2,1)S(1)}, bf16[14,4,1,512]{3,2,1,0:T(2,128)(2,1)S(1)}, u32[]{:S(2)}, u32[]{:S(2)}) collective-permute-start(bf16[14,4,1,512]{3,2,1,0:T(2,128)(2,1)S(1)} %get-tuple-element.15), channel_id=1, source_target_pairs={{0,1},{1,2},{2,3},{3,0},{4,5},{5,6},{6,7},{7,4},{8,9},{9,10},{10,1... | collective-permute-start | bytes 172040 | tf_op jit(solution)/shard_map/ppermute | solution.py:24
  41.9 5.1 %collective-permute-start.3 = (bf16[14,4,1,512]{3,2,1,0:T(2,128)(2,1)S(1)}, bf16[14,4,1,512]{3,2,1,0:T(2,128)(2,1)S(1)}, u32[]{:S(2)}, u32[]{:S(2)}) collective-permute-start(bf16[14,4,1,512]{3,2,1,0:T(2,128)(2,1)S(1)} %get-tuple-element.16), channel_id=1, source_target_pairs={{1,0},{2,1},{3,2},{0,3},{5,4},{6,5},{7,6},{4,7},{9,8},{10,9},{11,1... | collective-permute-start | bytes 172040 | tf_op jit(solution)/shard_map/ppermute | solution.py:26
  56.1 5.8 %copy-start.21 = (f32[512]{0:T(512)S(1)}, f32[512]{0:T(512)}, u32[]{:S(2)}) copy-start(f32[512]{0:T(512)} %param.19) | copy-start | bytes 6148
  56.1 5.8 %copy-start.22 = (f32[16]{0:T(128)S(1)}, f32[16]{0:T(128)}, u32[]{:S(2)}) copy-start(f32[16]{0:T(128)} %param.21) | copy-start | bytes 196
  56.1 6.3 %copy-start.19 = (f32[2,768]{1,0:T(2,128)S(1)}, f32[2,768]{1,0:T(2,128)}, u32[]{:S(2)}) copy-start(f32[2,768]{1,0:T(2,128)} %param.29) | copy-start | bytes 18436
  57.4 14.9 %all-to-all-start = ((f32[32,1,1152]{2,1,0:T(1,128)}), f32[32,1,1152]{2,1,0:T(1,128)S(1)}, u32[]{:S(2)}, u32[]{:S(2)}) async-start(f32[32,1,1152]{2,1,0:T(1,128)} %all_to_all.8), calls=%async_computation | async-start | bytes 294912 | tf_op jit(solution)/shard_map/all_to_all | solution.py:146
  72.3 3.2 copy-start.8
  72.3 3.2 copy-start.14
  376.1 1.1 slice-start
  400.8 3.7 copy-start.2
  412.3 4.9 %copy-start.1 = (bf16[3,512,512]{2,1,0:T(8,128)(2,1)S(1)}, bf16[3,512,512]{2,1,0:T(8,128)(2,1)}, u32[]{:S(2)}) copy-start(bf16[3,512,512]{2,1,0:T(8,128)(2,1)} %param.18) | copy-start | bytes 4718596
Sparse Core Ops, SparseCore 0:
  28.3 344.6 all-reduce.3

commit v2 on v0

v2 whole, which is shorter than its diff:
```python
import functools

import jax
import jax.numpy as jnp
from jax import lax
from jax.experimental import pallas as pl
from jax.experimental.pallas import tpu as pltpu
from jax.sharding import PartitionSpec as P

MESH = pl.DeviceIdType.MESH
F32 = jnp.float32
BF16 = jnp.bfloat16
HIGHEST = lax.Precision.HIGHEST

D = 6144
HD = 128
C = 512
LAT = 16
FR = 4
LANES = 128
GROUP = 16
N_FSDP = 32
N_CP = 4
WINDOWS = 4
ROWS = 12
COLS = 24
ROW_BLOCKS = 8
ROW_SPLIT = 2
COL_SPLIT = 4
PATCH = 3
CELLS = ROW_BLOCKS * PATCH * PATCH
WIDE = WINDOWS * COLS
PW_ROWS = 64
POS_ROWS = 48
TABLE_ROWS = PW_ROWS + 2 * POS_ROWS + GROUP
KEPT = PW_ROWS + TABLE_ROWS
GROUPS = TABLE_ROWS // GROUP
SHIFT_ROW = 11
HEAD_TILES = 18
PIECE = 7
TILES = N_FSDP * PIECE
OWN = D // N_FSDP


def split_2(values):
    high = values.astype(BF16)
    low = (values - high.astype(F32)).astype(BF16)
    return high, low


def place(shape):
    return [lax.broadcasted_iota(jnp.int32, shape, axis) for axis in range(len(shape))]


def token_coefs(cells, fsdp, column):
    group, row_part, col_part = fsdp // 8, fsdp // 4 % 2, fsdp % 4
    cell, lane = place((CELLS, LANES))
    block, inner = cell // 9, cell % 9
    row = block * 6 + row_part * PATCH + inner // PATCH
    col = column * 12 + col_part * PATCH + inner % PATCH
    base = (lane == row) | (lane == POS_ROWS + col)
    base = base | ((lane >= 2 * POS_ROWS + 8) & (lane < 2 * POS_ROWS + SHIFT_ROW))
    coefs = []
    for late in range(2):
        hot = base | (lane == 2 * POS_ROWS + group * 2 + late)
        kept = (lane // PW_ROWS) == late
        coefs.append(
            jnp.concatenate(
                [jnp.where(kept, cells, 0.0), jnp.where(hot, 1.0, 0.0)[:, : KEPT - LANES]],
                axis=1,
            )
        )
    return jnp.concatenate(coefs, axis=0).astype(BF16)


def exchange_kernel(
    video,
    conv_weight,
    conv_bias,
    time_weight,
    time_bias,
    latent_weight,
    latent_bias,
    patch_weight,
    patch_bias,
    frame_pos,
    row_pos,
    col_pos,
    modulation,
    weight,
    panel_out,
    cells_out,
    tables,
    video_in,
    conv_in,
    time_in,
    left_side,
    parts,
    arrived,
    piece,
    folded,
    kernels,
    q0,
    q1,
    q2,
    direct,
    edge_out,
    edge_in,
    padded,
    spread_out,
    messages,
    latents_in,
    sums,
    cells,
    embedded,
    token_out,
    local_sems,
    sums_sems,
    panel_sems,
    edge_send,
    edge_recv,
    tile_sems,
    cell_sems,
):
    me = lax.axis_index("fsdp")
    column = lax.axis_index("cp")
    barrier = pltpu.get_barrier_semaphore()

    def greet(step, carry):
        pl.semaphore_signal(
            barrier, inc=1, device_id={"fsdp": (me + step) % N_FSDP}, device_id_type=MESH
        )
        return carry

    lax.fori_loop(1, N_FSDP, greet, 0)
    for step in range(1, N_CP):
        pl.semaphore_signal(
            barrier, inc=1, device_id={"cp": (column + step) % N_CP}, device_id_type=MESH
        )
    loads = [
        pltpu.make_async_copy(source, target, local_sems.at[at])
        for at, (source, target) in enumerate(
            [
                (patch_weight, tables.at[pl.ds(PW_ROWS, PW_ROWS)]),
                (row_pos, tables.at[pl.ds(2 * PW_ROWS, POS_ROWS)]),
                (col_pos, tables.at[pl.ds(2 * PW_ROWS + POS_ROWS, POS_ROWS)]),
                (time_weight, time_in),
                (conv_weight, conv_in),
                (video, video_in),
                (patch_weight, tables.at[pl.ds(0, PW_ROWS)]),
            ]
        )
    ]
    for load in loads:
        load.start()

    bias = patch_bias[...]
    bias_high = bias.astype(BF16).astype(F32)
    bias_mid = (bias - bias_high).astype(BF16).astype(F32)
    bias_low = bias - bias_high - bias_mid
    eight = lax.broadcasted_iota(jnp.int32, (8, D), 0)
    tail = jnp.where(
        eight == 0,
        bias_high,
        jnp.where(eight == 1, bias_mid, jnp.where(eight == 2, bias_low, 0.0)),
    )
    tables[pl.ds(KEPT - GROUP, GROUP), :] = jnp.concatenate(
        [frame_pos[...].astype(F32), tail], axis=0
    ).astype(BF16)
    for load in loads[:3]:
        load.wait()
    start = pl.multiple_of((me // 2) * (2 * OWN), 2 * OWN)
    odd = me % 2 == 1
    own_mod = modulation[:, pl.ds(start, 2 * OWN)]
    own_scale = 1.0 + own_mod[0:1]
    own_shift = own_mod[1:2]

    def scaled(group, carry):
        at = pl.multiple_of(PW_ROWS + group * GROUP, GROUP)
        whole = tables[pl.ds(at, GROUP), :].astype(F32)
        center = jnp.sum(whole, axis=1, keepdims=True) * (1.0 / D)
        block = tables[pl.ds(at, GROUP), pl.ds(start, 2 * OWN)].astype(F32)
        block = (block - center) * own_scale
        row = lax.broadcasted_iota(jnp.int32, block.shape, 0)
        block = jnp.where((row == SHIFT_ROW) & (group == GROUPS - 1), own_shift, block)
        block = jnp.where(odd, block[:, OWN:], block[:, :OWN])
        high, low = split_2(block)
        to = pl.multiple_of(group * GROUP, GROUP)
        left_side[pl.ds(to, GROUP), :] = high
        left_side[pl.ds(TABLE_ROWS + to, GROUP), :] = low
        return carry

    lax.fori_loop(0, GROUPS, scaled, 0)
    for which in range(3):
        for pair in range(3):
            part = jnp.dot(
                left_side[...],
                weight[which, :, pair * 256 : (pair + 1) * 256],
                preferred_element_type=F32,
            )
            part = part[:TABLE_ROWS] + part[TABLE_ROWS:]
            for half in range(2):
                tile = which * 6 + pair * 2 + half
                parts[pl.ds(tile * GROUPS, GROUPS)] = (
                    part[:, half * LANES : (half + 1) * LANES]
                    .astype(BF16)
                    .reshape(GROUPS, GROUP, LANES)
                )
    spare = TILES - HEAD_TILES * GROUPS
    parts[pl.ds(HEAD_TILES * GROUPS, spare)] = jnp.zeros((spare, GROUP, LANES), BF16)
    pl.semaphore_wait(barrier, N_FSDP - 1 + N_CP - 1)

    def part_copy(step):
        target = (me + step) % N_FSDP
        return pltpu.make_async_remote_copy(
            src_ref=parts.at[pl.ds(target * PIECE, PIECE)],
            dst_ref=arrived.at[N_FSDP - 1 - step],
            send_sem=sums_sems.at[0],
            recv_sem=sums_sems.at[1],
            device_id={"fsdp": target},
            device_id_type=MESH,
        )

    def send_part(step, carry):
        part_copy(step).start()
        return carry

    lax.fori_loop(1, N_FSDP, send_part, 0)

    frame = (me + N_FSDP - 4) % N_FSDP // ROW_BLOCKS
    channel, lane = place((LAT, LANES))
    latent_in = latent_weight[...]

    def spread(keep):
        return jnp.dot(
            latent_in, jnp.where(keep, 1.0, 0.0).astype(BF16), preferred_element_type=F32
        ).astype(BF16)

    early_index = jnp.minimum(frame + 1, 2)
    late_index = jnp.maximum(frame - 1, 0)
    early_keep = (frame <= 1) & (lane == channel)
    late_keep = (frame >= 1) & (lane == PW_ROWS + channel)
    loads[3].wait()
    both = jnp.dot(time_in[early_index], spread(early_keep), preferred_element_type=F32)
    both = both + jnp.dot(time_in[late_index], spread(late_keep), preferred_element_type=F32)
    high, low = split_2(both)
    folded[:, :LANES] = high
    folded[:, LANES:] = low
    bias_row = jnp.dot(conv_bias[...], both, precision=HIGHEST, preferred_element_type=F32)
    loads[4].wait()

    def fold(col_shift, carry):
        total = None
        for row_shift in range(3):
            through = jnp.dot(
                conv_in[row_shift, col_shift], folded[...], preferred_element_type=F32
            )
            through = through[:, :LANES] + through[:, LANES:]
            if row_shift:
                through = pltpu.roll(through, row_shift * LAT, 1)
            total = through if total is None else total + through
        high, low = split_2(total)
        kernels[col_shift, :, :LANES] = high
        kernels[col_shift, :, LANES:] = low
        return carry

    lax.fori_loop(0, 3, fold, 0)
    loads[5].wait()

    def convolve(row, carry):
        at = pl.multiple_of(row * WIDE, WIDE)
        raw = video_in[pl.ds(at, WIDE), :]
        wide = raw.astype(F32)
        active = (wide / (1.0 + jnp.exp(-wide))).astype(BF16)
        for col_shift, kept in enumerate((q0, q1, q2)):
            through = jnp.dot(active, kernels[col_shift], preferred_element_type=F32)
            kept[pl.ds(at, WIDE), :] = through[:, :LANES] + through[:, LANES:]
        plain = jnp.dot(raw, folded[...], preferred_element_type=F32)
        direct[pl.ds(at, WIDE), :] = plain[:, :LANES] + plain[:, LANES:] + bias_row
        return carry

    lax.fori_loop(0, ROWS, convolve, 0)
    lines = ROWS * WINDOWS
    edge_out[0] = q0[pl.ds(COLS - 1, lines, stride=COLS), :]
    edge_out[1] = q2[pl.ds(0, lines, stride=COLS), :]
    edges = [
        pltpu.make_async_remote_copy(
            src_ref=edge_out.at[side],
            dst_ref=edge_in.at[side],
            send_sem=edge_send.at[side],
            recv_sem=edge_recv.at[side],
            device_id={"cp": (column + step) % N_CP},
            device_id_type=MESH,
        )
        for side, step in ((0, 1), (1, N_CP - 1))
    ]
    for edge in edges:
        edge.start()
    empty = jnp.zeros((2 * WIDE, LANES), F32)
    padded[pl.ds(0, 2 * WIDE), :] = empty
    padded[pl.ds((ROWS + 2) * WIDE, 2 * WIDE), :] = empty
    pixel = lax.broadcasted_iota(jnp.int32, (WIDE, LANES), 0) % COLS

    def columns(row, carry):
        at = pl.multiple_of(row * WIDE, WIDE)
        here = pl.ds(at, WIDE)
        total = q1[here, :]
        total = total + jnp.where(pixel == 0, 0.0, pltpu.roll(q0[here, :], 1, 0))
        total = total + jnp.where(pixel == COLS - 1, 0.0, pltpu.roll(q2[here, :], WIDE - 1, 0))
        padded[pl.ds(pl.multiple_of(at + 2 * WIDE, WIDE), WIDE), :] = total
        return carry

    lax.fori_loop(0, ROWS, columns, 0)
    for edge in edges:
        edge.wait()
    first = pl.ds(2 * WIDE, lines, stride=COLS)
    last = pl.ds(2 * WIDE + COLS - 1, lines, stride=COLS)
    padded[first, :] = padded[first, :] + jnp.where(column > 0, edge_in[0], 0.0)
    padded[last, :] = padded[last, :] + jnp.where(column < N_CP - 1, edge_in[1], 0.0)
    own_lanes = lax.broadcasted_iota(jnp.int32, (WIDE, LANES), 1) % PW_ROWS < LAT

    def packed(row, parity):
        total = padded[pl.ds((row + 1) * WIDE, WIDE), :]
        total = total + pltpu.roll(
            padded[pl.ds((row + 2) * WIDE, WIDE), :], LANES - LAT, 1
        )
        total = total + pltpu.roll(
            padded[pl.ds((row + 3) * WIDE, WIDE), :], LANES - 2 * LAT, 1
        )
        if 0 <= row < ROWS:
            total = total + direct[pl.ds(row * WIDE, WIDE), :]
        spread_out[...] = jnp.where(own_lanes, total, 0.0)
        result = None
        for side in range(2):
            taken = spread_out[pl.ds(side, WIDE // 2, stride=2), :]
            shift = 2 * LAT * parity + LAT * side
            taken = pltpu.roll(taken, shift, 1) if shift else taken
            result = taken if result is None else result + taken
        return result

    def post(values, row_part, at):
        for window in range(WINDOWS):
            for part in range(COL_SPLIT):
                begin = window * COLS // 2 + part * PATCH
                messages[window * 8 + row_part * 4 + part, at : at + PATCH, :] = values[
                    begin : begin + PATCH
                ]

    messages[...] = jnp.zeros(messages.shape, F32)
    for pair in range(ROWS // 2):
        values = packed(2 * pair, 0) + packed(2 * pair + 1, 1)
        post(values, pair // PATCH, pair % PATCH * PATCH)
    post(packed(ROWS, 0), 0, PATCH * PATCH)
    post(packed(-1, 1), 1, PATCH * PATCH)
    slot = (me + N_FSDP - 4) % N_FSDP

    def tile_copy(step):
        target = (me + step) % N_FSDP
        return pltpu.make_async_remote_copy(
            src_ref=messages.at[target],
            dst_ref=latents_in.at[slot],
            send_sem=tile_sems.at[0],
            recv_sem=tile_sems.at[1],
            device_id={"fsdp": target},
            device_id_type=MESH,
        )

    def send_tile(step, carry):
        tile_copy(step).start()
        return carry

    lax.fori_loop(1, N_FSDP, send_tile, 0)
    latents_in[slot] = messages[me]

    def wait_all(ref, sem):
        view = ref.at[pl.ds(0, N_FSDP - 1)]
        pltpu.make_async_copy(view, view, sem).wait()

    wait_all(arrived, sums_sems.at[1])

    def add(step, total):
        return total + arrived[step].astype(F32)

    own = parts[pl.ds(me * PIECE, PIECE)].astype(F32)
    piece[...] = lax.fori_loop(0, N_FSDP - 1, add, own).astype(BF16)

    def panel_copy(step):
        return pltpu.make_async_remote_copy(
            src_ref=piece,
            dst_ref=panel_out.at[me],
            send_sem=panel_sems.at[0],
            recv_sem=panel_sems.at[1],
            device_id={"fsdp": (me + step) % N_FSDP},
            device_id_type=MESH,
        )

    def send_panel(step, carry):
        panel_copy(step).start()
        return carry

    lax.fori_loop(1, N_FSDP, send_panel, 0)
    panel_out[me] = piece[...]

    spread_all = spread(lane % LAT == channel).astype(F32)
    offset = jnp.dot(time_bias[...], spread_all, precision=HIGHEST, preferred_element_type=F32)
    offset = offset + jnp.dot(
        latent_bias[...],
        jnp.where(lane % LAT == channel, 1.0, 0.0),
        precision=HIGHEST,
        preferred_element_type=F32,
    )
    wait_all(latents_in, tile_sems.at[1])
    for block in range(ROW_BLOCKS):
        total = latents_in[block]
        for other in range(1, FR):
            total = total + latents_in[other * ROW_BLOCKS + block]
        sums[block] = total
    row_part = me // 4 % 2
    upper = jnp.where(row_part == 0, 1.0, 0.0)
    lower = 1.0 - upper
    nine = PATCH * PATCH
    for block in range(ROW_BLOCKS):
        cells[pl.ds(block * nine, nine), :] = sums[block, 0:nine, :]
        if block > 0:
            here = pl.ds(block * nine, PATCH)
            cells[here, :] = cells[here, :] + sums[block - 1, nine : nine + PATCH, :] * upper
        if block < ROW_BLOCKS - 1:
            here = pl.ds(block * nine + 2 * PATCH, PATCH)
            cells[here, :] = cells[here, :] + sums[block + 1, nine : nine + PATCH, :] * lower
    patches = (cells[...] + offset).astype(BF16).astype(F32)
    loads[6].wait()
    coefs = token_coefs(patches, me, column)
    wide = 512
    count = 2 * CELLS

    def embed(step, total):
        here = pl.ds(pl.multiple_of(step * wide, wide), wide)
        values = jnp.dot(coefs, tables[:, here], preferred_element_type=F32)
        embedded[:, here] = values
        return total + jnp.sum(values, axis=1, keepdims=True)

    center = lax.fori_loop(0, D // wide, embed, jnp.zeros((count, 1), F32)) * (1.0 / D)

    def deviate(step, total):
        here = pl.ds(pl.multiple_of(step * wide, wide), wide)
        values = embedded[:, here] - center
        return total + jnp.sum(values * values, axis=1, keepdims=True)

    spread_sum = lax.fori_loop(0, D // wide, deviate, jnp.zeros((count, 1), F32))
    scale = lax.rsqrt(spread_sum * (1.0 / D) + 1e-06)
    cell_lane = lax.broadcasted_iota(jnp.int32, (CELLS, LANES), 1)
    token_out[pl.ds(0, CELLS), :] = patches
    token_out[pl.ds(CELLS, CELLS), :] = jnp.where(
        cell_lane < PW_ROWS, scale[:CELLS], scale[CELLS:]
    )
    copies = [
        pltpu.make_async_remote_copy(
            src_ref=token_out,
            dst_ref=cells_out.at[column],
            send_sem=cell_sems.at[0],
            recv_sem=cell_sems.at[1],
            device_id={"cp": (column + step) % N_CP},
            device_id_type=MESH,
        )
        for step in range(1, N_CP)
    ]
    for copy in copies:
        copy.start()
    cells_out[column] = token_out[...]
    others = cells_out.at[pl.ds(0, N_CP - 1)]
    pltpu.make_async_copy(others, others, cell_sems.at[1]).wait()
    pltpu.make_async_copy(others, others, cell_sems.at[0]).wait()
    wait_all(arrived, sums_sems.at[0])
    wait_all(latents_in, tile_sems.at[0])
    wait_all(panel_out, panel_sems.at[0])
    wait_all(panel_out, panel_sems.at[1])


def exchange(*args):
    whole = pl.BlockSpec(memory_space=pltpu.VMEM)
    apart = pl.BlockSpec(memory_space=pl.ANY)
    in_specs = [
        apart,
        apart,
        whole,
        apart,
        whole,
        whole,
        whole,
        apart,
        whole,
        whole,
        apart,
        apart,
        whole,
        whole,
    ]
    pixels = ROWS * WIDE
    return pl.pallas_call(
        exchange_kernel,
        out_shape=(
            jax.ShapeDtypeStruct((N_FSDP, PIECE, GROUP, LANES), BF16),
            jax.ShapeDtypeStruct((N_CP, 2 * CELLS, LANES), F32),
        ),
        in_specs=in_specs,
        out_specs=(whole, whole),
        scratch_shapes=[
            pltpu.VMEM((KEPT, D), BF16),
            pltpu.VMEM((pixels, C), BF16),
            pltpu.VMEM((3, 3, C, C), BF16),
            pltpu.VMEM((3, C, C), BF16),
            pltpu.VMEM((2 * TABLE_ROWS, OWN), BF16),
            pltpu.VMEM((TILES, GROUP, LANES), BF16),
            pltpu.VMEM((N_FSDP - 1, PIECE, GROUP, LANES), BF16),
            pltpu.VMEM((PIECE, GROUP, LANES), BF16),
            pltpu.VMEM((C, 2 * LANES), BF16),
            pltpu.VMEM((3, C, 2 * LANES), BF16),
            pltpu.VMEM((pixels, LANES), F32),
            pltpu.VMEM((pixels, LANES), F32),
            pltpu.VMEM((pixels, LANES), F32),
            pltpu.VMEM((pixels, LANES), F32),
            pltpu.VMEM((2, ROWS * WINDOWS, LANES), F32),
            pltpu.VMEM((2, ROWS * WINDOWS, LANES), F32),
            pltpu.VMEM(((ROWS + 4) * WIDE, LANES), F32),
            pltpu.VMEM((WIDE, LANES), F32),
            pltpu.VMEM((N_FSDP, GROUP, LANES), F32),
            pltpu.VMEM((N_FSDP, GROUP, LANES), F32),
            pltpu.VMEM((ROW_BLOCKS, GROUP, LANES), F32),
            pltpu.VMEM((CELLS, LANES), F32),
            pltpu.VMEM((2 * CELLS, D), F32),
            pltpu.VMEM((2 * CELLS, LANES), F32),
            pltpu.SemaphoreType.DMA((7,)),
            pltpu.SemaphoreType.DMA((2,)),
            pltpu.SemaphoreType.DMA((2,)),
            pltpu.SemaphoreType.DMA((2,)),
            pltpu.SemaphoreType.DMA((2,)),
            pltpu.SemaphoreType.DMA((2,)),
            pltpu.SemaphoreType.DMA((2,)),
        ],
        compiler_params=pltpu.CompilerParams(
            collective_id=0, has_side_effects=True, vmem_limit_bytes=48 * 1024 * 1024
        ),
    )(*args)


def project_kernel(cells, panel, gain, query, keys, values, coefs, scales):
    me = lax.axis_index("fsdp")
    step = pl.program_id(0)
    count = 2 * CELLS

    @pl.when(step == 0)
    def _():
        for column in range(N_CP):
            both = cells[column]
            coefs[pl.ds(column * count, count), :] = token_coefs(both[:CELLS], me, column)
            scale = both[CELLS:]
            lane = lax.broadcasted_iota(jnp.int32, scale.shape, 1)
            turned = pltpu.roll(scale, PW_ROWS, 1)
            scales[pl.ds(column * count, CELLS), :] = jnp.where(lane < PW_ROWS, scale, turned)
            scales[pl.ds(column * count + CELLS, CELLS), :] = jnp.where(
                lane < PW_ROWS, turned, scale
            )

    for which, out in enumerate((query, keys, values)):
        sides = []
        for half in range(2):
            tile = which * 6 + step * 2 + half
            rows = panel[pl.ds(pl.multiple_of(tile * TABLE_ROWS, GROUP), TABLE_ROWS), :]
            sides.append(rows)
        both = jnp.concatenate(sides, axis=1)
        stacked = jnp.concatenate([both[:PW_ROWS], both], axis=0)
        shift_at = TABLE_ROWS - GROUP
        shift = both[shift_at:].astype(F32)[SHIFT_ROW : SHIFT_ROW + 1]
        for column in range(N_CP):
            here = pl.ds(column * count, count)
            projected = jnp.dot(coefs[here, :], stacked, preferred_element_type=F32)
            scale = scales[here, :]
            for half in range(2):
                side = slice(half * LANES, (half + 1) * LANES)
                part = projected[:, side] * scale + shift[:, side]
                if which < 2:
                    power = jnp.sum(part * part, axis=1, keepdims=True) * (1.0 / HD)
                    part = part * lax.rsqrt(power + 1e-06) * gain[which : which + 1, side]
                out[here, side] = part.astype(BF16)


def project(cells, panel, gain, tokens):
    width = 2 * LANES
    out = jax.ShapeDtypeStruct((tokens, gain.shape[1]), BF16)
    block = pl.BlockSpec((tokens, width), lambda step: (0, step))
    return pl.pallas_call(
        project_kernel,
        grid=(3,),
        out_shape=(out, out, out),
        in_specs=[
            pl.BlockSpec(cells.shape, lambda step: (0, 0, 0)),
            pl.BlockSpec(panel.shape, lambda step: (0, 0)),
            pl.BlockSpec((2, width), lambda step: (0, step)),
        ],
        out_specs=(block, block, block),
        scratch_shapes=[
            pltpu.VMEM((tokens, KEPT), BF16),
            pltpu.VMEM((tokens, LANES), F32),
        ],
        compiler_params=pltpu.CompilerParams(vmem_limit_bytes=32 * 1024 * 1024),
    )(cells, panel, gain)


def body(
    video,
    conv_weight,
    conv_bias,
    time_weight,
    time_bias,
    latent_weight,
    latent_bias,
    patch_weight,
    patch_bias,
    frame_pos,
    row_pos,
    col_pos,
    modulation,
    qkv_weight,
    qk_gain,
):
    panel, cells = exchange(
        video.reshape(-1, C),
        conv_weight,
        conv_bias.reshape(1, -1),
        time_weight,
        time_bias.reshape(1, -1),
        latent_weight,
        latent_bias.reshape(1, -1),
        patch_weight,
        patch_bias.reshape(1, -1),
        frame_pos,
        row_pos,
        col_pos,
        modulation,
        qkv_weight,
    )
    return project(cells, panel.reshape(-1, LANES), qk_gain, N_CP * 2 * CELLS)


def solution(mesh):
    return jax.shard_map(
        body,
        mesh=mesh,
        in_specs=(
            P("fsdp", None, "cp", None),
            P(),
            P(),
            P(),
            P(),
            P(),
            P(),
            P(),
            P(),
            P(),
            P(),
            P(),
            P(),
            P(None, "fsdp", "cp"),
            P(None, "cp"),
        ),
        out_specs=(P("fsdp", "cp"), P("fsdp", "cp"), P("fsdp", "cp")),
        check_vma=False,
    )
```

time: 471 us -> 60.6 us (0.13)
  the two profiles are of different devices: /device:TPU:0 before, /device:TPU:1 now
where the time goes in v2:
time: 60.6 us; the launch traced here: 60 us
  Pallas kernels  48.3 us (80%)
  local copies, waits for them, and re-layouts  11 us (18%)
  between operations  0.67 us (1%)
    pallas_call x1, Pallas kernels, exchange(): pl.pallas_call(exchange_kernel, out_shape=(jax.ShapeDtypeStruct((N_FSDP,...  45.2 us
    unnamed x25, local copies, waits for them, and re-layouts  11 us
    pallas_call x1, Pallas kernels, project(): pl.pallas_call(project_kernel, grid=(3,), out_shape=(out, out, out), in_s...  3.14 us

profile of v2, /device:TPU:1, one launch (start us, length us, event | category | flops | bytes accessed | tf_op | source)
XLA Modules:
  0.0 60.0 jit_solution(1277156403390156585)
XLA Ops:
  0.6 0.8 %copy.18.latent_weight = bf16[512,16]{1,0:T(8,128)(2,1)S(1)} copy(bf16[512,16]{0,1:T(8,128)(2,1)} %param.20) | data formatting | bytes 32768 | tf_op args[5]
  1.5 0.0 copy-start
  1.5 1.3 %copy-done = bf16[12,4,24,512]{3,2,1,0:T(8,128)(2,1)S(1)} copy-done((bf16[12,4,24,512]{3,2,1,0:T(8,128)(2,1)S(1)}, bf16[12,4,24,512]{3,2,1,0:T(8,128)(2,1)}, u32[]{:S(2)}) %copy-start) | copy-done | bytes 1179672
  2.7 0.0 copy-start.1
  2.7 1.2 %copy-done.1 = bf16[3,192,768]{2,1,0:T(8,128)(2,1)S(1)} copy-done((bf16[3,192,768]{2,1,0:T(8,128)(2,1)S(1)}, bf16[3,192,768]{2,1,0:T(8,128)(2,1)}, u32[]{:S(2)}) %copy-start.1) | copy-done | bytes 884760
  3.9 0.0 copy-start.2
  3.9 1.1 %copy-done.2 = bf16[64,6144]{1,0:T(8,128)(2,1)S(1)} copy-done((bf16[64,6144]{1,0:T(8,128)(2,1)S(1)}, bf16[64,6144]{1,0:T(8,128)(2,1)}, u32[]{:S(2)}) %copy-start.2) | copy-done | bytes 786456
  5.0 0.0 copy-start.3
  5.1 1.1 %copy-done.3 = bf16[48,6144]{1,0:T(8,128)(2,1)S(1)} copy-done((bf16[48,6144]{1,0:T(8,128)(2,1)S(1)}, bf16[48,6144]{1,0:T(8,128)(2,1)}, u32[]{:S(2)}) %copy-start.3) | copy-done | bytes 589848
  6.1 0.0 copy-start.4
  6.1 1.1 %copy-done.4 = bf16[48,6144]{1,0:T(8,128)(2,1)S(1)} copy-done((bf16[48,6144]{1,0:T(8,128)(2,1)S(1)}, bf16[48,6144]{1,0:T(8,128)(2,1)}, u32[]{:S(2)}) %copy-start.4) | copy-done | bytes 589848
  7.2 0.0 copy-start.5
  7.2 0.9 %copy-done.5 = bf16[8,6144]{1,0:T(8,128)(2,1)S(1)} copy-done((bf16[8,6144]{1,0:T(8,128)(2,1)S(1)}, bf16[8,6144]{1,0:T(8,128)(2,1)}, u32[]{:S(2)}) %copy-start.5) | copy-done | bytes 98328
  8.1 0.0 copy-start.6
  8.1 0.8 %copy-done.6 = f32[2,6144]{1,0:T(2,128)S(1)} copy-done((f32[2,6144]{1,0:T(2,128)S(1)}, f32[2,6144]{1,0:T(2,128)}, u32[]{:S(2)}) %copy-start.6) | copy-done | bytes 49176
  8.9 0.0 copy-start.7
  8.9 0.7 %copy-done.7 = f32[6144]{0:T(1024)S(1)} copy-done((f32[6144]{0:T(1024)S(1)}, f32[6144]{0:T(1024)}, u32[]{:S(2)}) %copy-start.7) | copy-done | bytes 24600
  9.6 0.0 copy-start.9
  9.6 0.7 %copy-done.9 = f32[512]{0:T(512)S(1)} copy-done((f32[512]{0:T(512)S(1)}, f32[512]{0:T(512)}, u32[]{:S(2)}) %copy-start.9) | copy-done | bytes 2072
  10.3 0.0 copy-start.10
  10.3 0.7 %copy-done.10 = f32[512]{0:T(512)S(1)} copy-done((f32[512]{0:T(512)S(1)}, f32[512]{0:T(512)}, u32[]{:S(2)}) %copy-start.10) | copy-done | bytes 2072
  11.0 0.0 copy-start.11
  11.0 0.7 %copy-done.11 = f32[16]{0:T(128)S(1)} copy-done((f32[16]{0:T(128)S(1)}, f32[16]{0:T(128)}, u32[]{:S(2)}) %copy-start.11) | copy-done | bytes 88
  11.6 0.0 copy-start.8
  11.6 45.2 %shard_map.166 = (bf16[32,7,16,128]{3,2,1,0:T(8,128)(2,1)S(1)}, f32[4,144,128]{2,1,0:T(8,128)S(1)}) custom-call(bf16[1152,512]{1,0:T(8,128)(2,1)S(1)} %bitcast.6, bf16[3,3,512,512]{3,2,1,0:T(8,128)(2,1)} %conv_weight.1, f32[1,512]{1,0:T(1,128)S(1)} %bitcast.9, bf16[3,512,512]{2,1,0:T(8,128)(2,1)} %time_weight.1, f32[1,512]{1,0:T(1,128)S(1)} %bitcast.10, ...), custom_call_target="tpu_custom_call" | custom-call | tf_op jit(solution)/shard_map/pallas_call | solution.py:499
  56.8 0.0 copy-done.8
  56.8 3.1 %shard_map.167 = (bf16[576,768]{1,0:T(8,128)(2,1)}, bf16[576,768]{1,0:T(8,128)(2,1)}, bf16[576,768]{1,0:T(8,128)(2,1)}) custom-call(f32[4,144,128]{2,1,0:T(8,128)S(1)} %get-tuple-element.5.cells, bf16[3584,128]{1,0:T(8,128)(2,1)S(1)} %bitcast.7, f32[2,768]{1,0:T(2,128)S(1)} %copy-done.8), custom_call_target="tpu_custom_call" | custom-call | tf_op jit(solution)/shard_map/pallas_call | solution.py:591
Async XLA Ops:
  1.5 1.3 %copy-start = (bf16[12,4,24,512]{3,2,1,0:T(8,128)(2,1)S(1)}, bf16[12,4,24,512]{3,2,1,0:T(8,128)(2,1)}, u32[]{:S(2)}) copy-start(bf16[12,4,24,512]{3,2,1,0:T(8,128)(2,1)} %param.15) | copy-start | bytes 3538948
  2.7 1.2 %copy-start.1 = (bf16[3,192,768]{2,1,0:T(8,128)(2,1)S(1)}, bf16[3,192,768]{2,1,0:T(8,128)(2,1)}, u32[]{:S(2)}) copy-start(bf16[3,192,768]{2,1,0:T(8,128)(2,1)} %weight.1) | copy-start | bytes 2654212
  3.9 1.1 %copy-start.2 = (bf16[64,6144]{1,0:T(8,128)(2,1)S(1)}, bf16[64,6144]{1,0:T(8,128)(2,1)}, u32[]{:S(2)}) copy-start(bf16[64,6144]{1,0:T(8,128)(2,1)} %patch_weight.1) | copy-start | bytes 2359300
  5.0 1.1 %copy-start.3 = (bf16[48,6144]{1,0:T(8,128)(2,1)S(1)}, bf16[48,6144]{1,0:T(8,128)(2,1)}, u32[]{:S(2)}) copy-start(bf16[48,6144]{1,0:T(8,128)(2,1)} %row_pos.1) | copy-start | bytes 1769476
  6.1 1.1 %copy-start.4 = (bf16[48,6144]{1,0:T(8,128)(2,1)S(1)}, bf16[48,6144]{1,0:T(8,128)(2,1)}, u32[]{:S(2)}) copy-start(bf16[48,6144]{1,0:T(8,128)(2,1)} %col_pos.1) | copy-start | bytes 1769476
  7.2 0.9 %copy-start.5 = (bf16[8,6144]{1,0:T(8,128)(2,1)S(1)}, bf16[8,6144]{1,0:T(8,128)(2,1)}, u32[]{:S(2)}) copy-start(bf16[8,6144]{1,0:T(8,128)(2,1)} %frame_pos.1) | copy-start | bytes 294916
  8.1 0.8 %copy-start.6 = (f32[2,6144]{1,0:T(2,128)S(1)}, f32[2,6144]{1,0:T(2,128)}, u32[]{:S(2)}) copy-start(f32[2,6144]{1,0:T(2,128)} %modulation.1) | copy-start | bytes 147460
  8.9 0.7 %copy-start.7 = (f32[6144]{0:T(1024)S(1)}, f32[6144]{0:T(1024)}, u32[]{:S(2)}) copy-start(f32[6144]{0:T(1024)} %param.23) | copy-start | bytes 73732
  9.6 0.7 %copy-start.9 = (f32[512]{0:T(512)S(1)}, f32[512]{0:T(512)}, u32[]{:S(2)}) copy-start(f32[512]{0:T(512)} %param.17) | copy-start | bytes 6148
  10.3 0.7 %copy-start.10 = (f32[512]{0:T(512)S(1)}, f32[512]{0:T(512)}, u32[]{:S(2)}) copy-start(f32[512]{0:T(512)} %param.19) | copy-start | bytes 6148
  11.0 0.7 %copy-start.11 = (f32[16]{0:T(128)S(1)}, f32[16]{0:T(128)}, u32[]{:S(2)}) copy-start(f32[16]{0:T(128)} %param.21) | copy-start | bytes 196
  11.6 45.2 %copy-start.8 = (f32[2,768]{1,0:T(2,128)S(1)}, f32[2,768]{1,0:T(2,128)}, u32[]{:S(2)}) copy-start(f32[2,768]{1,0:T(2,128)} %gain.1) | copy-start | bytes 18436

commit v3 on v2

--- a/solution.py
+++ b/solution.py
@@ -37,8 +37,13 @@
 GROUPS = TABLE_ROWS // GROUP
 SHIFT_ROW = 11
 HEAD_TILES = 18
-PIECE = 7
-TILES = N_FSDP * PIECE
+HALF_TILES = HEAD_TILES // 2 * GROUPS
+QUARTER = 25
+SMALL = 4
+RING = 4
+NEAR = 8
+CELL_ROWS = 80
+CHUNK = 4 * 96
 OWN = D // N_FSDP
 
 
@@ -74,30 +79,43 @@
 
 
 def exchange_kernel(
-    video,
-    conv_weight,
-    conv_bias,
-    time_weight,
-    time_bias,
-    latent_weight,
-    latent_bias,
-    patch_weight,
-    patch_bias,
-    frame_pos,
-    row_pos,
-    col_pos,
-    modulation,
-    weight,
+    video_far,
+    conv_far,
+    conv_bias_far,
+    time_far,
+    time_bias_far,
+    latent_weight_far,
+    latent_bias_far,
+    patch_weight_far,
+    patch_bias_far,
+    frame_pos_far,
+    row_pos_far,
+    col_pos_far,
+    modulation_far,
+    weight_far,
     panel_out,
     cells_out,
+    gram_out,
     tables,
     video_in,
     conv_in,
     time_in,
+    weight,
+    conv_bias,
+    time_bias,
+    latent_weight,
+    latent_bias,
+    patch_bias,
+    frame_pos,
+    modulation,
+    centers,
     left_side,
     parts,
-    arrived,
-    piece,
+    ring_in,
+    blocks,
+    near_in,
+    pieces,
+    gathered,
     folded,
     kernels,
     q0,
@@ -112,10 +130,11 @@
     latents_in,
     sums,
     cells,
-    embedded,
     token_out,
     local_sems,
-    sums_sems,
+    ring_sems,
+    near_sems,
+    spread_sems,
     panel_sems,
     edge_send,
     edge_recv,
@@ -125,6 +144,25 @@
     me = lax.axis_index("fsdp")
     column = lax.axis_index("cp")
     barrier = pltpu.get_barrier_semaphore()
+    z_at, x_at, y_at = me // 8, me // 4 % 2, me % 4
+
+    def ring_peer(half, step):
+        if half == 0:
+            return (z_at + step) % RING * 8 + me % 8
+        return me // 4 * 4 + (y_at + step) % RING
+
+    def near_at(half):
+        return me % 8 if half == 0 else z_at * 2 + x_at
+
+    def near_peer(half, target):
+        if half == 0:
+            return me // 8 * 8 + target
+        return target // 2 * 8 + target % 2 * 4 + y_at
+
+    ring_at = (z_at, y_at)
+
+    def wait_bytes(view, sem):
+        pltpu.make_async_copy(view, view, sem).wait()
 
     def greet(step, carry):
         pl.semaphore_signal(
@@ -137,23 +175,32 @@
         pl.semaphore_signal(
             barrier, inc=1, device_id={"cp": (column + step) % N_CP}, device_id_type=MESH
         )
+    pairs = [
+        (patch_weight_far, tables.at[pl.ds(PW_ROWS, PW_ROWS)]),
+        (row_pos_far, tables.at[pl.ds(2 * PW_ROWS, POS_ROWS)]),
+        (col_pos_far, tables.at[pl.ds(2 * PW_ROWS + POS_ROWS, POS_ROWS)]),
+        (frame_pos_far, frame_pos),
+        (patch_bias_far, patch_bias),
+        (modulation_far, modulation),
+        (weight_far, weight),
+        (latent_weight_far, latent_weight),
+        (conv_bias_far, conv_bias),
+        (time_bias_far, time_bias),
+        (latent_bias_far, latent_bias),
+        (time_far, time_in),
+        (conv_far, conv_in),
+        (video_far, video_in),
+        (patch_weight_far, tables.at[pl.ds(0, PW_ROWS)]),
+    ]
     loads = [
         pltpu.make_async_copy(source, target, local_sems.at[at])
-        for at, (source, target) in enumerate(
-            [
-                (patch_weight, tables.at[pl.ds(PW_ROWS, PW_ROWS)]),
-                (row_pos, tables.at[pl.ds(2 * PW_ROWS, POS_ROWS)]),
-                (col_pos, tables.at[pl.ds(2 * PW_ROWS + POS_ROWS, POS_ROWS)]),
-                (time_weight, time_in),
-                (conv_weight, conv_in),
-                (video, video_in),
-                (patch_weight, tables.at[pl.ds(0, PW_ROWS)]),
-            ]
-        )
+        for at, (source, target) in enumerate(pairs)
     ]
     for load in loads:
         load.start()
 
+    for load in loads[:7]:
+        load.wait()
     bias = patch_bias[...]
     bias_high = bias.astype(BF16).astype(F32)
     bias_mid = (bias - bias_high).astype(BF16).astype(F32)
@@ -167,8 +214,6 @@
     tables[pl.ds(KEPT - GROUP, GROUP), :] = jnp.concatenate(
         [frame_pos[...].astype(F32), tail], axis=0
     ).astype(BF16)
-    for load in loads[:3]:
-        load.wait()
     start = pl.multiple_of((me // 2) * (2 * OWN), 2 * OWN)
     odd = me % 2 == 1
     own_mod = modulation[:, pl.ds(start, 2 * OWN)]
@@ -179,6 +224,7 @@
         at = pl.multiple_of(PW_ROWS + group * GROUP, GROUP)
         whole = tables[pl.ds(at, GROUP), :].astype(F32)
         center = jnp.sum(whole, axis=1, keepdims=True) * (1.0 / D)
+        centers[pl.ds(at, GROUP), :] = jnp.broadcast_to(center, (GROUP, LANES))
         block = tables[pl.ds(at, GROUP), pl.ds(start, 2 * OWN)].astype(F32)
         block = (block - center) * own_scale
         row = lax.broadcasted_iota(jnp.int32, block.shape, 0)
@@ -201,53 +247,58 @@
             part = part[:TABLE_ROWS] + part[TABLE_ROWS:]
             for half in range(2):
                 tile = which * 6 + pair * 2 + half
-                parts[pl.ds(tile * GROUPS, GROUPS)] = (
+                at = tile % 9 * GROUPS
+                parts[tile // 9, pl.ds(at, GROUPS)] = (
                     part[:, half * LANES : (half + 1) * LANES]
                     .astype(BF16)
                     .reshape(GROUPS, GROUP, LANES)
                 )
-    spare = TILES - HEAD_TILES * GROUPS
-    parts[pl.ds(HEAD_TILES * GROUPS, spare)] = jnp.zeros((spare, GROUP, LANES), BF16)
+    parts[:, HALF_TILES:] = jnp.zeros((2, 1, GROUP, LANES), BF16)
     pl.semaphore_wait(barrier, N_FSDP - 1 + N_CP - 1)
 
-    def part_copy(step):
-        target = (me + step) % N_FSDP
-        return pltpu.make_async_remote_copy(
-            src_ref=parts.at[pl.ds(target * PIECE, PIECE)],
-            dst_ref=arrived.at[N_FSDP - 1 - step],
-            send_sem=sums_sems.at[0],
-            recv_sem=sums_sems.at[1],
-            device_id={"fsdp": target},
-            device_id_type=MESH,
-        )
-
-    def send_part(step, carry):
-        part_copy(step).start()
-        return carry
-
-    lax.fori_loop(1, N_FSDP, send_part, 0)
+    ring_copies = []
+    for step in (2, 1, 3):
+        for half in range(2):
+            target = (ring_at[half] + step) % RING
+            ring_copies.append(
+                pltpu.make_async_remote_copy(
+                    src_ref=parts.at[half, pl.ds(target * QUARTER, QUARTER)],
+                    dst_ref=ring_in.at[half, RING - 1 - step],
+                    send_sem=ring_sems.at[half],
+                    recv_sem=ring_sems.at[2 + half],
+                    device_id={"fsdp": ring_peer(half, step)},
+                    device_id_type=MESH,
+                )
+            )
+    for copy in ring_copies:
+        copy.start()
 
     frame = (me + N_FSDP - 4) % N_FSDP // ROW_BLOCKS
     channel, lane = place((LAT, LANES))
+    for load in loads[7:11]:
+        load.wait()
     latent_in = latent_weight[...]
 
     def spread(keep):
-        return jnp.dot(
-            latent_in, jnp.where(keep, 1.0, 0.0).astype(BF16), preferred_element_type=F32
+        return lax.dot_general(
+            latent_in,
+            jnp.where(keep, 1.0, 0.0).astype(BF16),
+            (((0,), (0,)), ((), ())),
+            preferred_element_type=F32,
         ).astype(BF16)
 
     early_index = jnp.minimum(frame + 1, 2)
     late_index = jnp.maximum(frame - 1, 0)
     early_keep = (frame <= 1) & (lane == channel)
     late_keep = (frame >= 1) & (lane == PW_ROWS + channel)
-    loads[3].wait()
+    loads[11].wait()
     both = jnp.dot(time_in[early_index], spread(early_keep), preferred_element_type=F32)
     both = both + jnp.dot(time_in[late_index], spread(late_keep), preferred_element_type=F32)
     high, low = split_2(both)
     folded[:, :LANES] = high
     folded[:, LANES:] = low
     bias_row = jnp.dot(conv_bias[...], both, precision=HIGHEST, preferred_element_type=F32)
-    loads[4].wait()
+    loads[12].wait()
 
     def fold(col_shift, carry):
         total = None
@@ -265,21 +316,21 @@
         return carry
 
     lax.fori_loop(0, 3, fold, 0)
-    loads[5].wait()
+    loads[13].wait()
 
     def convolve(row, carry):
-        at = pl.multiple_of(row * WIDE, WIDE)
-        raw = video_in[pl.ds(at, WIDE), :]
+        at = pl.multiple_of(row * CHUNK, CHUNK)
+        raw = video_in[pl.ds(at, CHUNK), :]
         wide = raw.astype(F32)
         active = (wide / (1.0 + jnp.exp(-wide))).astype(BF16)
         for col_shift, kept in enumerate((q0, q1, q2)):
             through = jnp.dot(active, kernels[col_shift], preferred_element_type=F32)
-            kept[pl.ds(at, WIDE), :] = through[:, :LANES] + through[:, LANES:]
+            kept[pl.ds(at, CHUNK), :] = through[:, :LANES] + through[:, LANES:]
         plain = jnp.dot(raw, folded[...], preferred_element_type=F32)
-        direct[pl.ds(at, WIDE), :] = plain[:, :LANES] + plain[:, LANES:] + bias_row
+        direct[pl.ds(at, CHUNK), :] = plain[:, :LANES] + plain[:, LANES:] + bias_row
         return carry
 
-    lax.fori_loop(0, ROWS, convolve, 0)
+    lax.fori_loop(0, ROWS * WIDE // CHUNK, convolve, 0)
     lines = ROWS * WINDOWS
     edge_out[0] = q0[pl.ds(COLS - 1, lines, stride=COLS), :]
     edge_out[1] = q2[pl.ds(0, lines, stride=COLS), :]
@@ -296,6 +347,30 @@
     ]
     for edge in edges:
         edge.start()
+    near_copies = []
+    for half in range(2):
+        wait_bytes(ring_in.at[half], ring_sems.at[2 + half])
+        total = parts[half, pl.ds(ring_at[half] * QUARTER, QUARTER)].astype(F32)
+        for other in range(RING - 1):
+            total = total + ring_in[half, other].astype(F32)
+        blocks[half, pl.ds(0, QUARTER)] = total.astype(BF16)
+        spare = NEAR * SMALL - QUARTER
+        blocks[half, pl.ds(QUARTER, spare)] = jnp.zeros((spare, GROUP, LANES), BF16)
+    for step in range(NEAR - 1, 0, -1):
+        for half in range(2):
+            target = (near_at(half) + step) % NEAR
+            near_copies.append(
+                pltpu.make_async_remote_copy(
+                    src_ref=blocks.at[half, pl.ds(target * SMALL, SMALL)],
+                    dst_ref=near_in.at[half, NEAR - 1 - step],
+                    send_sem=near_sems.at[half],
+                    recv_sem=near_sems.at[2 + half],
+                    device_id={"fsdp": near_peer(half, target)},
+                    device_id_type=MESH,
+                )
+            )
+    for copy in near_copies:
+        copy.start()
     empty = jnp.zeros((2 * WIDE, LANES), F32)
     padded[pl.ds(0, 2 * WIDE), :] = empty
     padded[pl.ds((ROWS + 2) * WIDE, 2 * WIDE), :] = empty
@@ -372,34 +447,61 @@
     lax.fori_loop(1, N_FSDP, send_tile, 0)
     latents_in[slot] = messages[me]
 
-    def wait_all(ref, sem):
-        view = ref.at[pl.ds(0, N_FSDP - 1)]
-        pltpu.make_async_copy(view, view, sem).wait()
-
-    wait_all(arrived, sums_sems.at[1])
-
-    def add(step, total):
-        return total + arrived[step].astype(F32)
-
-    own = parts[pl.ds(me * PIECE, PIECE)].astype(F32)
-    piece[...] = lax.fori_loop(0, N_FSDP - 1, add, own).astype(BF16)
-
-    def panel_copy(step):
-        return pltpu.make_async_remote_copy(
-            src_ref=piece,
-            dst_ref=panel_out.at[me],
-            send_sem=panel_sems.at[0],
-            recv_sem=panel_sems.at[1],
-            device_id={"fsdp": (me + step) % N_FSDP},
-            device_id_type=MESH,
-        )
-
-    def send_panel(step, carry):
-        panel_copy(step).start()
+    spread_copies = []
+    for half in range(2):
+        wait_bytes(near_in.at[half], near_sems.at[2 + half])
+        total = blocks[half, pl.ds(near_at(half) * SMALL, SMALL)].astype(F32)
+        for other in range(NEAR - 1):
+            total = total + near_in[half, other].astype(F32)
+        pieces[half] = total.astype(BF16)
+        gathered[half, pl.ds(near_at(half) * SMALL, SMALL)] = pieces[half]
+    for step in range(NEAR - 1, 0, -1):
+        for half in range(2):
+            spread_copies.append(
+                pltpu.make_async_remote_copy(
+                    src_ref=pieces.at[half],
+                    dst_ref=gathered.at[half, pl.ds(near_at(half) * SMALL, SMALL)],
+                    send_sem=spread_sems.at[half],
+                    recv_sem=spread_sems.at[2 + half],
+                    device_id={"fsdp": near_peer(half, (near_at(half) + step) % NEAR)},
+                    device_id_type=MESH,
+                )
+            )
+    for copy in spread_copies:
+        copy.start()
+
+    loads[14].wait()
+    centers[pl.ds(0, PW_ROWS), :] = centers[pl.ds(PW_ROWS, PW_ROWS), :]
+    gram_out[...] = jnp.zeros((KEPT, KEPT), F32)
+    both_last = (((1,), (1,)), ((), ()))
+
+    def product(step, carry):
+        here = pl.ds(pl.multiple_of(step * 1024, 1024), 1024)
+        high, low = split_2(tables[:, here].astype(F32) - centers[:, :1])
+        total = lax.dot_general(high, high, both_last, preferred_element_type=F32)
+        cross = lax.dot_general(high, low, both_last, preferred_element_type=F32)
+        gram_out[...] += (total + 2.0 * cross) * (1.0 / D)
         return carry
 
-    lax.fori_loop(1, N_FSDP, send_panel, 0)
-    panel_out[me] = piece[...]
+    lax.fori_loop(0, D // 1024, product, 0)
+    panel_copies = []
+    for half in range(2):
+        wait_bytes(gathered.at[half, pl.ds(0, (NEAR - 1) * SMALL)], spread_sems.at[2 + half])
+        at = half * RING * QUARTER + ring_at[half] * QUARTER
+        for step in (2, 1, 3):
+            panel_copies.append(
+                pltpu.make_async_remote_copy(
+                    src_ref=gathered.at[half, pl.ds(0, QUARTER)],
+                    dst_ref=panel_out.at[pl.ds(at, QUARTER)],
+                    send_sem=panel_sems.at[half],
+                    recv_sem=panel_sems.at[2 + half],
+                    device_id={"fsdp": ring_peer(half, step)},
+                    device_id_type=MESH,
+                )
+            )
+        for copy in panel_copies[-3:]:
+            copy.start()
+        panel_out[pl.ds(at, QUARTER)] = gathered[half, pl.ds(0, QUARTER)]
 
     spread_all = spread(lane % LAT == channel).astype(F32)
     offset = jnp.dot(time_bias[...], spread_all, precision=HIGHEST, preferred_element_type=F32)
@@ -409,7 +511,7 @@
         precision=HIGHEST,
         preferred_element_type=F32,
     )
-    wait_all(latents_in, tile_sems.at[1])
+    wait_bytes(latents_in.at[pl.ds(0, N_FSDP - 1)], tile_sems.at[1])
     for block in range(ROW_BLOCKS):
         total = latents_in[block]
         for other in range(1, FR):
@@ -427,32 +529,8 @@
         if block < ROW_BLOCKS - 1:
             here = pl.ds(block * nine + 2 * PATCH, PATCH)
             cells[here, :] = cells[here, :] + sums[block + 1, nine : nine + PATCH, :] * lower
-    patches = (cells[...] + offset).astype(BF16).astype(F32)
-    loads[6].wait()
-    coefs = token_coefs(patches, me, column)
-    wide = 512
-    count = 2 * CELLS
-
-    def embed(step, total):
-        here = pl.ds(pl.multiple_of(step * wide, wide), wide)
-        values = jnp.dot(coefs, tables[:, here], preferred_element_type=F32)
-        embedded[:, here] = values
-        return total + jnp.sum(values, axis=1, keepdims=True)
-
-    center = lax.fori_loop(0, D // wide, embed, jnp.zeros((count, 1), F32)) * (1.0 / D)
-
-    def deviate(step, total):
-        here = pl.ds(pl.multiple_of(step * wide, wide), wide)
-        values = embedded[:, here] - center
-        return total + jnp.sum(values * values, axis=1, keepdims=True)
-
-    spread_sum = lax.fori_loop(0, D // wide, deviate, jnp.zeros((count, 1), F32))
-    scale = lax.rsqrt(spread_sum * (1.0 / D) + 1e-06)
-    cell_lane = lax.broadcasted_iota(jnp.int32, (CELLS, LANES), 1)
-    token_out[pl.ds(0, CELLS), :] = patches
-    token_out[pl.ds(CELLS, CELLS), :] = jnp.where(
-        cell_lane < PW_ROWS, scale[:CELLS], scale[CELLS:]
-    )
+    cells[pl.ds(CELLS, CELL_ROWS - CELLS), :] = jnp.zeros((CELL_ROWS - CELLS, LANES), F32)
+    token_out[...] = (cells[...] + offset).astype(BF16)
     copies = [
         pltpu.make_async_remote_copy(
             src_ref=token_out,
@@ -468,51 +546,52 @@
         copy.start()
     cells_out[column] = token_out[...]
     others = cells_out.at[pl.ds(0, N_CP - 1)]
-    pltpu.make_async_copy(others, others, cell_sems.at[1]).wait()
-    pltpu.make_async_copy(others, others, cell_sems.at[0]).wait()
-    wait_all(arrived, sums_sems.at[0])
-    wait_all(latents_in, tile_sems.at[0])
-    wait_all(panel_out, panel_sems.at[0])
-    wait_all(panel_out, panel_sems.at[1])
+    wait_bytes(others, cell_sems.at[1])
+    wait_bytes(others, cell_sems.at[0])
+    wait_bytes(latents_in.at[pl.ds(0, N_FSDP - 1)], tile_sems.at[0])
+    for half in range(2):
+        wait_bytes(ring_in.at[half], ring_sems.at[half])
+        wait_bytes(near_in.at[half], near_sems.at[half])
+        wait_bytes(gathered.at[half, pl.ds(0, (NEAR - 1) * SMALL)], spread_sems.at[half])
+        sent = panel_out.at[pl.ds(0, (RING - 1) * QUARTER)]
+        wait_bytes(sent, panel_sems.at[half])
+        wait_bytes(sent, panel_sems.at[2 + half])
 
 
 def exchange(*args):
     whole = pl.BlockSpec(memory_space=pltpu.VMEM)
-    apart = pl.BlockSpec(memory_space=pl.ANY)
-    in_specs = [
-        apart,
-        apart,
-        whole,
-        apart,
-        whole,
-        whole,
-        whole,
-        apart,
-        whole,
-        whole,
-        apart,
-        apart,
-        whole,
-        whole,
-    ]
+    apart = pl.BlockSpec(memory_space=pltpu.HBM)
     pixels = ROWS * WIDE
     return pl.pallas_call(
         exchange_kernel,
         out_shape=(
-            jax.ShapeDtypeStruct((N_FSDP, PIECE, GROUP, LANES), BF16),
-            jax.ShapeDtypeStruct((N_CP, 2 * CELLS, LANES), F32),
+            jax.ShapeDtypeStruct((2 * RING * QUARTER, GROUP, LANES), BF16),
+            jax.ShapeDtypeStruct((N_CP, CELL_ROWS, LANES), BF16),
+            jax.ShapeDtypeStruct((KEPT, KEPT), F32),
         ),
-        in_specs=in_specs,
-        out_specs=(whole, whole),
+        in_specs=[apart] * len(args),
+        out_specs=(whole, whole, whole),
         scratch_shapes=[
             pltpu.VMEM((KEPT, D), BF16),
             pltpu.VMEM((pixels, C), BF16),
             pltpu.VMEM((3, 3, C, C), BF16),
             pltpu.VMEM((3, C, C), BF16),
+            pltpu.VMEM((3, OWN, 6 * LANES), BF16),
+            pltpu.VMEM((1, C), F32),
+            pltpu.VMEM((1, C), F32),
+            pltpu.VMEM((LAT, C), BF16),
+            pltpu.VMEM((1, LAT), F32),
+            pltpu.VMEM((1, D), F32),
+            pltpu.VMEM((8, D), BF16),
+            pltpu.VMEM((2, D), F32),
+            pltpu.VMEM((KEPT, LANES), F32),
             pltpu.VMEM((2 * TABLE_ROWS, OWN), BF16),
-            pltpu.VMEM((TILES, GROUP, LANES), BF16),
-            pltpu.VMEM((N_FSDP - 1, PIECE, GROUP, LANES), BF16),
-            pltpu.VMEM((PIECE, GROUP, LANES), BF16),
+            pltpu.VMEM((2, RING * QUARTER, GROUP, LANES), BF16),
+            pltpu.VMEM((2, RING - 1, QUARTER, GROUP, LANES), BF16),
+            pltpu.VMEM((2, NEAR * SMALL, GROUP, LANES), BF16),
+            pltpu.VMEM((2, NEAR - 1, SMALL, GROUP, LANES), BF16),
+            pltpu.VMEM((2, SMALL, GROUP, LANES), BF16),
+            pltpu.VMEM((2, NEAR * SMALL, GROUP, LANES), BF16),
             pltpu.VMEM((C, 2 * LANES), BF16),
             pltpu.VMEM((3, C, 2 * LANES), BF16),
             pltpu.VMEM((pixels, LANES), F32),
@@ -526,12 +605,13 @@
             pltpu.VMEM((N_FSDP, GROUP, LANES), F32),
             pltpu.VMEM((N_FSDP, GROUP, LANES), F32),
             pltpu.VMEM((ROW_BLOCKS, GROUP, LANES), F32),
-            pltpu.VMEM((CELLS, LANES), F32),
-            pltpu.VMEM((2 * CELLS, D), F32),
-            pltpu.VMEM((2 * CELLS, LANES), F32),
-            pltpu.SemaphoreType.DMA((7,)),
-            pltpu.SemaphoreType.DMA((2,)),
-            pltpu.SemaphoreType.DMA((2,)),
+            pltpu.VMEM((CELL_ROWS, LANES), F32),
+            pltpu.VMEM((CELL_ROWS, LANES), BF16),
+            pltpu.SemaphoreType.DMA((15,)),
+            pltpu.SemaphoreType.DMA((4,)),
+            pltpu.SemaphoreType.DMA((4,)),
+            pltpu.SemaphoreType.DMA((4,)),
+            pltpu.SemaphoreType.DMA((4,)),
             pltpu.SemaphoreType.DMA((2,)),
             pltpu.SemaphoreType.DMA((2,)),
             pltpu.SemaphoreType.DMA((2,)),
@@ -540,32 +620,33 @@
         compiler_params=pltpu.CompilerParams(
             collective_id=0, has_side_effects=True, vmem_limit_bytes=48 * 1024 * 1024
         ),
-    )(*args)
-
-
-def project_kernel(cells, panel, gain, query, keys, values, coefs, scales):
+    )(*[pltpu.with_memory_space_constraint(arg, pltpu.HBM) for arg in args])
+
+
+def project_kernel(cells, panel, gram, gain, query, keys, values, coefs, scales):
     me = lax.axis_index("fsdp")
     step = pl.program_id(0)
     count = 2 * CELLS
 
     @pl.when(step == 0)
     def _():
+        high, low = split_2(gram[...])
         for column in range(N_CP):
-            both = cells[column]
-            coefs[pl.ds(column * count, count), :] = token_coefs(both[:CELLS], me, column)
-            scale = both[CELLS:]
-            lane = lax.broadcasted_iota(jnp.int32, scale.shape, 1)
-            turned = pltpu.roll(scale, PW_ROWS, 1)
-            scales[pl.ds(column * count, CELLS), :] = jnp.where(lane < PW_ROWS, scale, turned)
-            scales[pl.ds(column * count + CELLS, CELLS), :] = jnp.where(
-                lane < PW_ROWS, turned, scale
-            )
+            here = pl.ds(column * count, count)
+            own = token_coefs(cells[column].astype(F32)[:CELLS], me, column)
+            coefs[here, :] = own
+            through = jnp.dot(own, high, preferred_element_type=F32)
+            through = through + jnp.dot(own, low, preferred_element_type=F32)
+            power = jnp.sum(through * own.astype(F32), axis=1, keepdims=True)
+            scale = lax.rsqrt(jnp.maximum(power, 0.0) + 1e-06)
+            scales[here, :] = jnp.broadcast_to(scale, (count, LANES))
 
     for which, out in enumerate((query, keys, values)):
         sides = []
         for half in range(2):
             tile = which * 6 + step * 2 + half
-            rows = panel[pl.ds(pl.multiple_of(tile * TABLE_ROWS, GROUP), TABLE_ROWS), :]
+            at = tile * TABLE_ROWS + jnp.where(tile >= HEAD_TILES // 2, GROUP, 0)
+            rows = panel[pl.ds(pl.multiple_of(at, GROUP), TABLE_ROWS), :]
             sides.append(rows)
         both = jnp.concatenate(sides, axis=1)
         stacked = jnp.concatenate([both[:PW_ROWS], both], axis=0)
@@ -584,7 +665,7 @@
                 out[here, side] = part.astype(BF16)
 
 
-def project(cells, panel, gain, tokens):
+def project(cells, panel, gram, gain, tokens):
     width = 2 * LANES
     out = jax.ShapeDtypeStruct((tokens, gain.shape[1]), BF16)
     block = pl.BlockSpec((tokens, width), lambda step: (0, step))
@@ -595,6 +676,7 @@
         in_specs=[
             pl.BlockSpec(cells.shape, lambda step: (0, 0, 0)),
             pl.BlockSpec(panel.shape, lambda step: (0, 0)),
+            pl.BlockSpec(gram.shape, lambda step: (0, 0)),
             pl.BlockSpec((2, width), lambda step: (0, step)),
         ],
         out_specs=(block, block, block),
@@ -603,7 +685,7 @@
             pltpu.VMEM((tokens, LANES), F32),
         ],
         compiler_params=pltpu.CompilerParams(vmem_limit_bytes=32 * 1024 * 1024),
-    )(cells, panel, gain)
+    )(cells, panel, gram, gain)
 
 
 def body(
@@ -623,13 +705,13 @@
     qkv_weight,
     qk_gain,
 ):
-    panel, cells = exchange(
+    panel, cells, gram = exchange(
         video.reshape(-1, C),
         conv_weight,
         conv_bias.reshape(1, -1),
         time_weight,
         time_bias.reshape(1, -1),
-        latent_weight,
+        latent_weight.T,
         latent_bias.reshape(1, -1),
         patch_weight,
         patch_bias.reshape(1, -1),
@@ -639,7 +721,7 @@
         modulation,
         qkv_weight,
     )
-    return project(cells, panel.reshape(-1, LANES), qk_gain, N_CP * 2 * CELLS)
+    return project(cells, panel.reshape(-1, LANES), gram, qk_gain, N_CP * 2 * CELLS)
 
 
 def solution(mesh):

time: 60.6 us -> 41.8 us (0.69)
  the two profiles are of different devices: /device:TPU:1 before, /device:TPU:0 now
where the time goes in v3:
time: 41.8 us; the launch traced here: 41.1 us
  Pallas kernels  40.4 us (97%)
  between operations  0.66 us (2%)
    pallas_call x1, Pallas kernels, exchange(): pl.pallas_call(exchange_kernel, out_shape=(jax.ShapeDtypeStruct((2 * RING...  37 us
    pallas_call x1, Pallas kernels, project(): pl.pallas_call(project_kernel, grid=(3,), out_shape=(out, out, out), in_s...  3.4 us

profile of v3, /device:TPU:0, one launch (start us, length us, event | category | flops | bytes accessed | tf_op | source)
XLA Modules:
  0.0 41.1 jit_solution(12504973473478576211)
XLA Ops:
  0.6 0.0 copy-start
  0.6 37.0 %shard_map.166 = (bf16[200,16,128]{2,1,0:T(8,128)(2,1)S(1)}, bf16[4,80,128]{2,1,0:T(8,128)(2,1)S(1)}, f32[240,240]{1,0:T(8,128)S(1)}) custom-call(bf16[1152,512]{1,0:T(8,128)(2,1)} %bitcast.8, bf16[3,3,512,512]{3,2,1,0:T(8,128)(2,1)} %conv_far.1, f32[1,512]{1,0:T(1,128)} %bitcast.11, bf16[3,512,512]{2,1,0:T(8,128)(2,1)} %time_far.1, f32[1,512]{1,0:T(1,128)} %bitcast.12, ...), custom_call_target="tpu_custom_call" | custom-call | tf_op jit(solution)/shard_map/pallas_call | solution.py:565
  37.6 0.0 copy-done
  37.6 3.4 %shard_map.167 = (bf16[576,768]{1,0:T(8,128)(2,1)}, bf16[576,768]{1,0:T(8,128)(2,1)}, bf16[576,768]{1,0:T(8,128)(2,1)}) custom-call(bf16[4,80,128]{2,1,0:T(8,128)(2,1)S(1)} %get-tuple-element.6.cells, bf16[3200,128]{1,0:T(8,128)(2,1)S(1)} %bitcast.7, f32[240,240]{1,0:T(8,128)S(1)} %get-tuple-element.8.gram, f32[2,768]{1,0:T(2,128)S(1)} %copy-done), custom_call_target="tpu_custom_call" | custom-call | tf_op jit(solution)/shard_map/pallas_call | solution.py:672
Async XLA Ops:
  0.6 37.0 %copy-start = (f32[2,768]{1,0:T(2,128)S(1)}, f32[2,768]{1,0:T(2,128)}, u32[]{:S(2)}) copy-start(f32[2,768]{1,0:T(2,128)} %gain.1) | copy-start | bytes 18436

commit v4 on v3

--- a/solution.py
+++ b/solution.py
@@ -93,9 +93,16 @@
     col_pos_far,
     modulation_far,
     weight_far,
+    gain_far,
+    query_out,
+    keys_out,
+    values_out,
     panel_out,
     cells_out,
     gram_out,
+    coefs,
+    scales,
+    gain,
     tables,
     video_in,
     conv_in,
@@ -126,6 +133,7 @@
     edge_in,
     padded,
     spread_out,
+    staged,
     messages,
     latents_in,
     sums,
@@ -164,17 +172,6 @@
     def wait_bytes(view, sem):
         pltpu.make_async_copy(view, view, sem).wait()
 
-    def greet(step, carry):
-        pl.semaphore_signal(
-            barrier, inc=1, device_id={"fsdp": (me + step) % N_FSDP}, device_id_type=MESH
-        )
-        return carry
-
-    lax.fori_loop(1, N_FSDP, greet, 0)
-    for step in range(1, N_CP):
-        pl.semaphore_signal(
-            barrier, inc=1, device_id={"cp": (column + step) % N_CP}, device_id_type=MESH
-        )
     pairs = [
         (patch_weight_far, tables.at[pl.ds(PW_ROWS, PW_ROWS)]),
         (row_pos_far, tables.at[pl.ds(2 * PW_ROWS, POS_ROWS)]),
@@ -187,6 +184,7 @@
         (conv_bias_far, conv_bias),
         (time_bias_far, time_bias),
         (latent_bias_far, latent_bias),
+        (gain_far, gain),
         (time_far, time_in),
         (conv_far, conv_in),
         (video_far, video_in),
@@ -199,6 +197,17 @@
     for load in loads:
         load.start()
 
+    def greet(step, carry):
+        pl.semaphore_signal(
+            barrier, inc=1, device_id={"fsdp": (me + step) % N_FSDP}, device_id_type=MESH
+        )
+        return carry
+
+    lax.fori_loop(1, N_FSDP, greet, 0)
+    for step in range(1, N_CP):
+        pl.semaphore_signal(
+            barrier, inc=1, device_id={"cp": (column + step) % N_CP}, device_id_type=MESH
+        )
     for load in loads[:7]:
         load.wait()
     bias = patch_bias[...]
@@ -220,23 +229,20 @@
     own_scale = 1.0 + own_mod[0:1]
     own_shift = own_mod[1:2]
 
-    def scaled(group, carry):
-        at = pl.multiple_of(PW_ROWS + group * GROUP, GROUP)
+    for group in range(GROUPS):
+        at = PW_ROWS + group * GROUP
         whole = tables[pl.ds(at, GROUP), :].astype(F32)
         center = jnp.sum(whole, axis=1, keepdims=True) * (1.0 / D)
         centers[pl.ds(at, GROUP), :] = jnp.broadcast_to(center, (GROUP, LANES))
         block = tables[pl.ds(at, GROUP), pl.ds(start, 2 * OWN)].astype(F32)
         block = (block - center) * own_scale
-        row = lax.broadcasted_iota(jnp.int32, block.shape, 0)
-        block = jnp.where((row == SHIFT_ROW) & (group == GROUPS - 1), own_shift, block)
+        if group == GROUPS - 1:
+            row = lax.broadcasted_iota(jnp.int32, block.shape, 0)
+            block = jnp.where(row == SHIFT_ROW, own_shift, block)
         block = jnp.where(odd, block[:, OWN:], block[:, :OWN])
         high, low = split_2(block)
-        to = pl.multiple_of(group * GROUP, GROUP)
-        left_side[pl.ds(to, GROUP), :] = high
-        left_side[pl.ds(TABLE_ROWS + to, GROUP), :] = low
-        return carry
-
-    lax.fori_loop(0, GROUPS, scaled, 0)
+        left_side[pl.ds(group * GROUP, GROUP), :] = high
+        left_side[pl.ds(TABLE_ROWS + group * GROUP, GROUP), :] = low
     for which in range(3):
         for pair in range(3):
             part = jnp.dot(
@@ -275,7 +281,7 @@
 
     frame = (me + N_FSDP - 4) % N_FSDP // ROW_BLOCKS
     channel, lane = place((LAT, LANES))
-    for load in loads[7:11]:
+    for load in loads[7:12]:
         load.wait()
     latent_in = latent_weight[...]
 
@@ -291,14 +297,14 @@
     late_index = jnp.maximum(frame - 1, 0)
     early_keep = (frame <= 1) & (lane == channel)
     late_keep = (frame >= 1) & (lane == PW_ROWS + channel)
-    loads[11].wait()
+    loads[12].wait()
     both = jnp.dot(time_in[early_index], spread(early_keep), preferred_element_type=F32)
     both = both + jnp.dot(time_in[late_index], spread(late_keep), preferred_element_type=F32)
     high, low = split_2(both)
     folded[:, :LANES] = high
     folded[:, LANES:] = low
     bias_row = jnp.dot(conv_bias[...], both, precision=HIGHEST, preferred_element_type=F32)
-    loads[12].wait()
+    loads[13].wait()
 
     def fold(col_shift, carry):
         total = None
@@ -316,7 +322,7 @@
         return carry
 
     lax.fori_loop(0, 3, fold, 0)
-    loads[13].wait()
+    loads[14].wait()
 
     def convolve(row, carry):
         at = pl.multiple_of(row * CHUNK, CHUNK)
@@ -347,7 +353,6 @@
     ]
     for edge in edges:
         edge.start()
-    near_copies = []
     for half in range(2):
         wait_bytes(ring_in.at[half], ring_sems.at[2 + half])
         total = parts[half, pl.ds(ring_at[half] * QUARTER, QUARTER)].astype(F32)
@@ -356,21 +361,16 @@
         blocks[half, pl.ds(0, QUARTER)] = total.astype(BF16)
         spare = NEAR * SMALL - QUARTER
         blocks[half, pl.ds(QUARTER, spare)] = jnp.zeros((spare, GROUP, LANES), BF16)
-    for step in range(NEAR - 1, 0, -1):
-        for half in range(2):
+        for step in range(NEAR - 1, 0, -1):
             target = (near_at(half) + step) % NEAR
-            near_copies.append(
-                pltpu.make_async_remote_copy(
-                    src_ref=blocks.at[half, pl.ds(target * SMALL, SMALL)],
-                    dst_ref=near_in.at[half, NEAR - 1 - step],
-                    send_sem=near_sems.at[half],
-                    recv_sem=near_sems.at[2 + half],
-                    device_id={"fsdp": near_peer(half, target)},
-                    device_id_type=MESH,
-                )
-            )
-    for copy in near_copies:
-        copy.start()
+            pltpu.make_async_remote_copy(
+                src_ref=blocks.at[half, pl.ds(target * SMALL, SMALL)],
+                dst_ref=near_in.at[half, NEAR - 1 - step],
+                send_sem=near_sems.at[half],
+                recv_sem=near_sems.at[2 + half],
+                device_id={"fsdp": near_peer(half, target)},
+                device_id_type=MESH,
+            ).start()
     empty = jnp.zeros((2 * WIDE, LANES), F32)
     padded[pl.ds(0, 2 * WIDE), :] = empty
     padded[pl.ds((ROWS + 2) * WIDE, 2 * WIDE), :] = empty
@@ -417,16 +417,17 @@
         for window in range(WINDOWS):
             for part in range(COL_SPLIT):
                 begin = window * COLS // 2 + part * PATCH
-                messages[window * 8 + row_part * 4 + part, at : at + PATCH, :] = values[
+                staged[window * 8 + row_part * 4 + part, at : at + PATCH, :] = values[
                     begin : begin + PATCH
                 ]
 
-    messages[...] = jnp.zeros(messages.shape, F32)
+    staged[...] = jnp.zeros(staged.shape, F32)
     for pair in range(ROWS // 2):
         values = packed(2 * pair, 0) + packed(2 * pair + 1, 1)
         post(values, pair // PATCH, pair % PATCH * PATCH)
     post(packed(ROWS, 0), 0, PATCH * PATCH)
     post(packed(-1, 1), 1, PATCH * PATCH)
+    messages[...] = staged[...].astype(BF16)
     slot = (me + N_FSDP - 4) % N_FSDP
 
     def tile_copy(step):
@@ -447,7 +448,6 @@
     lax.fori_loop(1, N_FSDP, send_tile, 0)
     latents_in[slot] = messages[me]
 
-    spread_copies = []
     for half in range(2):
         wait_bytes(near_in.at[half], near_sems.at[2 + half])
         total = blocks[half, pl.ds(near_at(half) * SMALL, SMALL)].astype(F32)
@@ -455,22 +455,17 @@
             total = total + near_in[half, other].astype(F32)
         pieces[half] = total.astype(BF16)
         gathered[half, pl.ds(near_at(half) * SMALL, SMALL)] = pieces[half]
-    for step in range(NEAR - 1, 0, -1):
-        for half in range(2):
-            spread_copies.append(
-                pltpu.make_async_remote_copy(
-                    src_ref=pieces.at[half],
-                    dst_ref=gathered.at[half, pl.ds(near_at(half) * SMALL, SMALL)],
-                    send_sem=spread_sems.at[half],
-                    recv_sem=spread_sems.at[2 + half],
-                    device_id={"fsdp": near_peer(half, (near_at(half) + step) % NEAR)},
-                    device_id_type=MESH,
-                )
-            )
-    for copy in spread_copies:
-        copy.start()
-
-    loads[14].wait()
+        for step in range(NEAR - 1, 0, -1):
+            pltpu.make_async_remote_copy(
+                src_ref=pieces.at[half],
+                dst_ref=gathered.at[half, pl.ds(near_at(half) * SMALL, SMALL)],
+                send_sem=spread_sems.at[half],
+                recv_sem=spread_sems.at[2 + half],
+                device_id={"fsdp": near_peer(half, (near_at(half) + step) % NEAR)},
+                device_id_type=MESH,
+            ).start()
+
+    loads[15].wait()
     centers[pl.ds(0, PW_ROWS), :] = centers[pl.ds(PW_ROWS, PW_ROWS), :]
     gram_out[...] = jnp.zeros((KEPT, KEPT), F32)
     both_last = (((1,), (1,)), ((), ()))
@@ -484,6 +479,7 @@
         return carry
 
     lax.fori_loop(0, D // 1024, product, 0)
+    gram_high, gram_low = split_2(gram_out[...])
     panel_copies = []
     for half in range(2):
         wait_bytes(gathered.at[half, pl.ds(0, (NEAR - 1) * SMALL)], spread_sems.at[2 + half])
@@ -513,9 +509,9 @@
     )
     wait_bytes(latents_in.at[pl.ds(0, N_FSDP - 1)], tile_sems.at[1])
     for block in range(ROW_BLOCKS):
-        total = latents_in[block]
+        total = latents_in[block].astype(F32)
         for other in range(1, FR):
-            total = total + latents_in[other * ROW_BLOCKS + block]
+            total = total + latents_in[other * ROW_BLOCKS + block].astype(F32)
         sums[block] = total
     row_part = me // 4 % 2
     upper = jnp.where(row_part == 0, 1.0, 0.0)
@@ -547,31 +543,69 @@
     cells_out[column] = token_out[...]
     others = cells_out.at[pl.ds(0, N_CP - 1)]
     wait_bytes(others, cell_sems.at[1])
+    count = 2 * CELLS
+    for group in range(N_CP):
+        here = pl.ds(group * count, count)
+        own = token_coefs(cells_out[group].astype(F32)[:CELLS], me, group)
+        coefs[here, :] = own
+        through = jnp.dot(own, gram_high, preferred_element_type=F32)
+        through = through + jnp.dot(own, gram_low, preferred_element_type=F32)
+        power = jnp.sum(through * own.astype(F32), axis=1, keepdims=True)
+        scale = lax.rsqrt(jnp.maximum(power, 0.0) + 1e-06)
+        scales[here, :] = jnp.broadcast_to(scale, (count, LANES))
+    sent = panel_out.at[pl.ds(0, (RING - 1) * QUARTER)]
+    for half, steps in enumerate(((0, 2, 4, 6, 8, 9), (9, 10, 12, 14, 16, 18))):
+        wait_bytes(sent, panel_sems.at[2 + half])
+        for begin, end in zip(steps[:-1], steps[1:]):
+            sides = []
+            for head in range(begin, end):
+                rows = panel_out[pl.ds(half + head * GROUPS, GROUPS)]
+                sides.append(rows.reshape(TABLE_ROWS, LANES))
+            both = jnp.concatenate(sides, axis=1)
+            stacked = jnp.concatenate([both[:PW_ROWS], both], axis=0)
+            tail_rows = both[TABLE_ROWS - GROUP :].astype(F32)
+            shift = tail_rows[SHIFT_ROW : SHIFT_ROW + 1]
+            for group in range(N_CP):
+                here = pl.ds(group * count, count)
+                projected = jnp.dot(coefs[here, :], stacked, preferred_element_type=F32)
+                for head in range(begin, end):
+                    from_lane = (head - begin) * LANES
+                    side = slice(from_lane, from_lane + LANES)
+                    which, to = head // 6, head % 6 * LANES
+                    part = projected[:, side] * scales[here, :] + shift[:, side]
+                    if which < 2:
+                        power = jnp.sum(part * part, axis=1, keepdims=True) * (1.0 / HD)
+                        part = part * lax.rsqrt(power + 1e-06)
+                        part = part * gain[which : which + 1, to : to + LANES]
+                    out = (query_out, keys_out, values_out)[which]
+                    out[here, to : to + LANES] = part.astype(BF16)
     wait_bytes(others, cell_sems.at[0])
     wait_bytes(latents_in.at[pl.ds(0, N_FSDP - 1)], tile_sems.at[0])
     for half in range(2):
         wait_bytes(ring_in.at[half], ring_sems.at[half])
         wait_bytes(near_in.at[half], near_sems.at[half])
         wait_bytes(gathered.at[half, pl.ds(0, (NEAR - 1) * SMALL)], spread_sems.at[half])
-        sent = panel_out.at[pl.ds(0, (RING - 1) * QUARTER)]
         wait_bytes(sent, panel_sems.at[half])
-        wait_bytes(sent, panel_sems.at[2 + half])
 
 
 def exchange(*args):
     whole = pl.BlockSpec(memory_space=pltpu.VMEM)
     apart = pl.BlockSpec(memory_space=pltpu.HBM)
     pixels = ROWS * WIDE
+    tokens = N_CP * 2 * CELLS
+    out = jax.ShapeDtypeStruct((tokens, 6 * LANES), BF16)
     return pl.pallas_call(
         exchange_kernel,
-        out_shape=(
-            jax.ShapeDtypeStruct((2 * RING * QUARTER, GROUP, LANES), BF16),
-            jax.ShapeDtypeStruct((N_CP, CELL_ROWS, LANES), BF16),
-            jax.ShapeDtypeStruct((KEPT, KEPT), F32),
-        ),
+        out_shape=(out, out, out),
         in_specs=[apart] * len(args),
         out_specs=(whole, whole, whole),
         scratch_shapes=[
+            pltpu.VMEM((2 * RING * QUARTER, GROUP, LANES), BF16),
+            pltpu.VMEM((N_CP, CELL_ROWS, LANES), BF16),
+            pltpu.VMEM((KEPT, KEPT), F32),
+            pltpu.VMEM((tokens, KEPT), BF16),
+            pltpu.VMEM((tokens, LANES), F32),
+            pltpu.VMEM((2, 6 * LANES), F32),
             pltpu.VMEM((KEPT, D), BF16),
             pltpu.VMEM((pixels, C), BF16),
             pltpu.VMEM((3, 3, C, C), BF16),
@@ -603,11 +637,12 @@
             pltpu.VMEM(((ROWS + 4) * WIDE, LANES), F32),
             pltpu.VMEM((WIDE, LANES), F32),
             pltpu.VMEM((N_FSDP, GROUP, LANES), F32),
-            pltpu.VMEM((N_FSDP, GROUP, LANES), F32),
+            pltpu.VMEM((N_FSDP, GROUP, LANES), BF16),
+            pltpu.VMEM((N_FSDP, GROUP, LANES), BF16),
             pltpu.VMEM((ROW_BLOCKS, GROUP, LANES), F32),
             pltpu.VMEM((CELL_ROWS, LANES), F32),
             pltpu.VMEM((CELL_ROWS, LANES), BF16),
-            pltpu.SemaphoreType.DMA((15,)),
+            pltpu.SemaphoreType.DMA((16,)),
             pltpu.SemaphoreType.DMA((4,)),
             pltpu.SemaphoreType.DMA((4,)),
             pltpu.SemaphoreType.DMA((4,)),
@@ -621,71 +656,6 @@
             collective_id=0, has_side_effects=True, vmem_limit_bytes=48 * 1024 * 1024
         ),
     )(*[pltpu.with_memory_space_constraint(arg, pltpu.HBM) for arg in args])
-
-
-def project_kernel(cells, panel, gram, gain, query, keys, values, coefs, scales):
-    me = lax.axis_index("fsdp")
-    step = pl.program_id(0)
-    count = 2 * CELLS
-
-    @pl.when(step == 0)
-    def _():
-        high, low = split_2(gram[...])
-        for column in range(N_CP):
-            here = pl.ds(column * count, count)
-            own = token_coefs(cells[column].astype(F32)[:CELLS], me, column)
-            coefs[here, :] = own
-            through = jnp.dot(own, high, preferred_element_type=F32)
-            through = through + jnp.dot(own, low, preferred_element_type=F32)
-            power = jnp.sum(through * own.astype(F32), axis=1, keepdims=True)
-            scale = lax.rsqrt(jnp.maximum(power, 0.0) + 1e-06)
-            scales[here, :] = jnp.broadcast_to(scale, (count, LANES))
-
-    for which, out in enumerate((query, keys, values)):
-        sides = []
-        for half in range(2):
-            tile = which * 6 + step * 2 + half
-            at = tile * TABLE_ROWS + jnp.where(tile >= HEAD_TILES // 2, GROUP, 0)
-            rows = panel[pl.ds(pl.multiple_of(at, GROUP), TABLE_ROWS), :]
-            sides.append(rows)
-        both = jnp.concatenate(sides, axis=1)
-        stacked = jnp.concatenate([both[:PW_ROWS], both], axis=0)
-        shift_at = TABLE_ROWS - GROUP
-        shift = both[shift_at:].astype(F32)[SHIFT_ROW : SHIFT_ROW + 1]
-        for column in range(N_CP):
-            here = pl.ds(column * count, count)
-            projected = jnp.dot(coefs[here, :], stacked, preferred_element_type=F32)
-            scale = scales[here, :]
-            for half in range(2):
-                side = slice(half * LANES, (half + 1) * LANES)
-                part = projected[:, side] * scale + shift[:, side]
-                if which < 2:
-                    power = jnp.sum(part * part, axis=1, keepdims=True) * (1.0 / HD)
-                    part = part * lax.rsqrt(power + 1e-06) * gain[which : which + 1, side]
-                out[here, side] = part.astype(BF16)
-
-
-def project(cells, panel, gram, gain, tokens):
-    width = 2 * LANES
-    out = jax.ShapeDtypeStruct((tokens, gain.shape[1]), BF16)
-    block = pl.BlockSpec((tokens, width), lambda step: (0, step))
-    return pl.pallas_call(
-        project_kernel,
-        grid=(3,),
-        out_shape=(out, out, out),
-        in_specs=[
-            pl.BlockSpec(cells.shape, lambda step: (0, 0, 0)),
-            pl.BlockSpec(panel.shape, lambda step: (0, 0)),
-            pl.BlockSpec(gram.shape, lambda step: (0, 0)),
-            pl.BlockSpec((2, width), lambda step: (0, step)),
-        ],
-        out_specs=(block, block, block),
-        scratch_shapes=[
-            pltpu.VMEM((tokens, KEPT), BF16),
-            pltpu.VMEM((tokens, LANES), F32),
-        ],
-        compiler_params=pltpu.CompilerParams(vmem_limit_bytes=32 * 1024 * 1024),
-    )(cells, panel, gram, gain)
 
 
 def body(
@@ -705,7 +675,7 @@
     qkv_weight,
     qk_gain,
 ):
-    panel, cells, gram = exchange(
+    results = exchange(
         video.reshape(-1, C),
         conv_weight,
         conv_bias.reshape(1, -1),
@@ -720,8 +690,9 @@
         col_pos,
         modulation,
         qkv_weight,
+        qk_gain,
     )
-    return project(cells, panel.reshape(-1, LANES), gram, qk_gain, N_CP * 2 * CELLS)
+    return results
 
 
 def solution(mesh):

time: 41.8 us -> 37.1 us (0.89); the launches traced: 41.1 us -> 37 us
  Pallas kernels: 40.4 us -> 33.6 us
  local copies, waits for them, and re-layouts: 0.01 us -> 2.74 us
    pallas_call x2 -> x1, Pallas kernels: 40.4 us -> 33.6 us  [exchange(): pl.pallas_call(exchange_kernel, out_shape=(out, out, out), in_specs=[apar...]
    unnamed x2 -> x3, local copies, waits for them, and re-layouts: 0.01 us -> 2.74 us
where the time goes in v4:
time: 37.1 us; the launch traced here: 37 us
  Pallas kernels  33.6 us (91%)
  local copies, waits for them, and re-layouts  2.74 us (7%)
  between operations  0.65 us (2%)
    pallas_call x1, Pallas kernels, exchange(): pl.pallas_call(exchange_kernel, out_shape=(out, out, out), in_specs=[apar...  33.6 us
    unnamed x3, local copies, waits for them, and re-layouts  2.74 us

profile of v4, /device:TPU:0, one launch (start us, length us, event | category | flops | bytes accessed | tf_op | source)
XLA Modules:
  0.0 37.0 jit_solution(6888724706178439279)
XLA Ops:
  0.6 33.6 %shard_map.166 = (bf16[576,768]{1,0:T(8,128)(2,1)S(1)}, bf16[576,768]{1,0:T(8,128)(2,1)S(1)}, bf16[576,768]{1,0:T(8,128)(2,1)S(1)}) custom-call(bf16[1152,512]{1,0:T(8,128)(2,1)} %bitcast.6, bf16[3,3,512,512]{3,2,1,0:T(8,128)(2,1)} %conv_far.1, f32[1,512]{1,0:T(1,128)} %bitcast.9, bf16[3,512,512]{2,1,0:T(8,128)(2,1)} %time_far.1, f32[1,512]{1,0:T(1,128)} %bitcast.10, ...), custom_call_target="tpu_custom_call" | custom-call | tf_op jit(solution)/shard_map/pallas_call | solution.py:597
  34.2 0.9 %copy.21 = bf16[576,768]{1,0:T(8,128)(2,1)} copy(bf16[576,768]{1,0:T(8,128)(2,1)S(1)} %get-tuple-element.6) | data formatting | bytes 1769472
  35.1 0.9 %copy.22 = bf16[576,768]{1,0:T(8,128)(2,1)} copy(bf16[576,768]{1,0:T(8,128)(2,1)S(1)} %get-tuple-element.7) | data formatting | bytes 1769472
  36.0 0.9 %copy.23 = bf16[576,768]{1,0:T(8,128)(2,1)} copy(bf16[576,768]{1,0:T(8,128)(2,1)S(1)} %get-tuple-element.8) | data formatting | bytes 1769472

commit v5 on v4

--- a/solution.py
+++ b/solution.py
@@ -93,16 +93,11 @@
     col_pos_far,
     modulation_far,
     weight_far,
-    gain_far,
-    query_out,
-    keys_out,
-    values_out,
     panel_out,
+    coefs,
+    scales,
     cells_out,
     gram_out,
-    coefs,
-    scales,
-    gain,
     tables,
     video_in,
     conv_in,
@@ -162,10 +157,15 @@
     def near_at(half):
         return me % 8 if half == 0 else z_at * 2 + x_at
 
-    def near_peer(half, target):
+    def near_peer(half, step):
+        x_to = (x_at + step[0]) % 2
         if half == 0:
-            return me // 8 * 8 + target
-        return target // 2 * 8 + target % 2 * 4 + y_at
+            ring_to = (y_at + step[1]) % RING
+            return x_to * RING + ring_to, z_at * 8 + x_to * 4 + ring_to
+        ring_to = (z_at + step[1]) % RING
+        return ring_to * 2 + x_to, ring_to * 8 + x_to * 4 + y_at
+
+    near_steps = ((1, 2), (1, 1), (1, 3), (0, 2), (1, 0), (0, 1), (0, 3))
 
     ring_at = (z_at, y_at)
 
@@ -184,7 +184,6 @@
         (conv_bias_far, conv_bias),
         (time_bias_far, time_bias),
         (latent_bias_far, latent_bias),
-        (gain_far, gain),
         (time_far, time_in),
         (conv_far, conv_in),
         (video_far, video_in),
@@ -281,7 +280,7 @@
 
     frame = (me + N_FSDP - 4) % N_FSDP // ROW_BLOCKS
     channel, lane = place((LAT, LANES))
-    for load in loads[7:12]:
+    for load in loads[7:11]:
         load.wait()
     latent_in = latent_weight[...]
 
@@ -297,14 +296,14 @@
     late_index = jnp.maximum(frame - 1, 0)
     early_keep = (frame <= 1) & (lane == channel)
     late_keep = (frame >= 1) & (lane == PW_ROWS + channel)
-    loads[12].wait()
+    loads[11].wait()
     both = jnp.dot(time_in[early_index], spread(early_keep), preferred_element_type=F32)
     both = both + jnp.dot(time_in[late_index], spread(late_keep), preferred_element_type=F32)
     high, low = split_2(both)
     folded[:, :LANES] = high
     folded[:, LANES:] = low
     bias_row = jnp.dot(conv_bias[...], both, precision=HIGHEST, preferred_element_type=F32)
-    loads[13].wait()
+    loads[12].wait()
 
     def fold(col_shift, carry):
         total = None
@@ -322,7 +321,7 @@
         return carry
 
     lax.fori_loop(0, 3, fold, 0)
-    loads[14].wait()
+    loads[13].wait()
 
     def convolve(row, carry):
         at = pl.multiple_of(row * CHUNK, CHUNK)
@@ -361,14 +360,14 @@
         blocks[half, pl.ds(0, QUARTER)] = total.astype(BF16)
         spare = NEAR * SMALL - QUARTER
         blocks[half, pl.ds(QUARTER, spare)] = jnp.zeros((spare, GROUP, LANES), BF16)
-        for step in range(NEAR - 1, 0, -1):
-            target = (near_at(half) + step) % NEAR
+        for slot, step in enumerate(near_steps):
+            target, peer = near_peer(half, step)
             pltpu.make_async_remote_copy(
                 src_ref=blocks.at[half, pl.ds(target * SMALL, SMALL)],
-                dst_ref=near_in.at[half, NEAR - 1 - step],
+                dst_ref=near_in.at[half, slot],
                 send_sem=near_sems.at[half],
                 recv_sem=near_sems.at[2 + half],
-                device_id={"fsdp": near_peer(half, target)},
+                device_id={"fsdp": peer},
                 device_id_type=MESH,
             ).start()
     empty = jnp.zeros((2 * WIDE, LANES), F32)
@@ -455,17 +454,17 @@
             total = total + near_in[half, other].astype(F32)
         pieces[half] = total.astype(BF16)
         gathered[half, pl.ds(near_at(half) * SMALL, SMALL)] = pieces[half]
-        for step in range(NEAR - 1, 0, -1):
+        for step in near_steps:
             pltpu.make_async_remote_copy(
                 src_ref=pieces.at[half],
                 dst_ref=gathered.at[half, pl.ds(near_at(half) * SMALL, SMALL)],
                 send_sem=spread_sems.at[half],
                 recv_sem=spread_sems.at[2 + half],
-                device_id={"fsdp": near_peer(half, (near_at(half) + step) % NEAR)},
+                device_id={"fsdp": near_peer(half, step)[1]},
                 device_id_type=MESH,
             ).start()
 
-    loads[15].wait()
+    loads[14].wait()
     centers[pl.ds(0, PW_ROWS), :] = centers[pl.ds(PW_ROWS, PW_ROWS), :]
     gram_out[...] = jnp.zeros((KEPT, KEPT), F32)
     both_last = (((1,), (1,)), ((), ()))
@@ -497,6 +496,8 @@
             )
         for copy in panel_copies[-3:]:
             copy.start()
+    for half in range(2):
+        at = half * RING * QUARTER + ring_at[half] * QUARTER
         panel_out[pl.ds(at, QUARTER)] = gathered[half, pl.ds(0, QUARTER)]
 
     spread_all = spread(lane % LAT == channel).astype(F32)
@@ -554,31 +555,8 @@
         scale = lax.rsqrt(jnp.maximum(power, 0.0) + 1e-06)
         scales[here, :] = jnp.broadcast_to(scale, (count, LANES))
     sent = panel_out.at[pl.ds(0, (RING - 1) * QUARTER)]
-    for half, steps in enumerate(((0, 2, 4, 6, 8, 9), (9, 10, 12, 14, 16, 18))):
+    for half in range(2):
         wait_bytes(sent, panel_sems.at[2 + half])
-        for begin, end in zip(steps[:-1], steps[1:]):
-            sides = []
-            for head in range(begin, end):
-                rows = panel_out[pl.ds(half + head * GROUPS, GROUPS)]
-                sides.append(rows.reshape(TABLE_ROWS, LANES))
-            both = jnp.concatenate(sides, axis=1)
-            stacked = jnp.concatenate([both[:PW_ROWS], both], axis=0)
-            tail_rows = both[TABLE_ROWS - GROUP :].astype(F32)
-            shift = tail_rows[SHIFT_ROW : SHIFT_ROW + 1]
-            for group in range(N_CP):
-                here = pl.ds(group * count, count)
-                projected = jnp.dot(coefs[here, :], stacked, preferred_element_type=F32)
-                for head in range(begin, end):
-                    from_lane = (head - begin) * LANES
-                    side = slice(from_lane, from_lane + LANES)
-                    which, to = head // 6, head % 6 * LANES
-                    part = projected[:, side] * scales[here, :] + shift[:, side]
-                    if which < 2:
-                        power = jnp.sum(part * part, axis=1, keepdims=True) * (1.0 / HD)
-                        part = part * lax.rsqrt(power + 1e-06)
-                        part = part * gain[which : which + 1, to : to + LANES]
-                    out = (query_out, keys_out, values_out)[which]
-                    out[here, to : to + LANES] = part.astype(BF16)
     wait_bytes(others, cell_sems.at[0])
     wait_bytes(latents_in.at[pl.ds(0, N_FSDP - 1)], tile_sems.at[0])
     for half in range(2):
@@ -593,19 +571,18 @@
     apart = pl.BlockSpec(memory_space=pltpu.HBM)
     pixels = ROWS * WIDE
     tokens = N_CP * 2 * CELLS
-    out = jax.ShapeDtypeStruct((tokens, 6 * LANES), BF16)
     return pl.pallas_call(
         exchange_kernel,
-        out_shape=(out, out, out),
+        out_shape=(
+            jax.ShapeDtypeStruct((2 * RING * QUARTER, GROUP, LANES), BF16),
+            jax.ShapeDtypeStruct((tokens, KEPT), BF16),
+            jax.ShapeDtypeStruct((tokens, LANES), F32),
+        ),
         in_specs=[apart] * len(args),
         out_specs=(whole, whole, whole),
         scratch_shapes=[
-            pltpu.VMEM((2 * RING * QUARTER, GROUP, LANES), BF16),
             pltpu.VMEM((N_CP, CELL_ROWS, LANES), BF16),
             pltpu.VMEM((KEPT, KEPT), F32),
-            pltpu.VMEM((tokens, KEPT), BF16),
-            pltpu.VMEM((tokens, LANES), F32),
-            pltpu.VMEM((2, 6 * LANES), F32),
             pltpu.VMEM((KEPT, D), BF16),
             pltpu.VMEM((pixels, C), BF16),
             pltpu.VMEM((3, 3, C, C), BF16),
@@ -642,7 +619,7 @@
             pltpu.VMEM((ROW_BLOCKS, GROUP, LANES), F32),
             pltpu.VMEM((CELL_ROWS, LANES), F32),
             pltpu.VMEM((CELL_ROWS, LANES), BF16),
-            pltpu.SemaphoreType.DMA((16,)),
+            pltpu.SemaphoreType.DMA((15,)),
             pltpu.SemaphoreType.DMA((4,)),
             pltpu.SemaphoreType.DMA((4,)),
             pltpu.SemaphoreType.DMA((4,)),
@@ -656,6 +633,59 @@
             collective_id=0, has_side_effects=True, vmem_limit_bytes=48 * 1024 * 1024
         ),
     )(*[pltpu.with_memory_space_constraint(arg, pltpu.HBM) for arg in args])
+
+
+def project_kernel(
+    panel, coefs, scales, gain, query, keys, values, results, result_sems
+):
+    count = 2 * CELLS
+    writes = []
+    for which, out in enumerate((query, keys, values)):
+        for pair in range(3):
+            sides = []
+            for head in range(which * 6 + pair * 2, which * 6 + pair * 2 + 2):
+                rows = panel[pl.ds(head // (HEAD_TILES // 2) + head * GROUPS, GROUPS)]
+                sides.append(rows.reshape(TABLE_ROWS, LANES))
+            both = jnp.concatenate(sides, axis=1)
+            stacked = jnp.concatenate([both[:PW_ROWS], both], axis=0)
+            tail_rows = both[TABLE_ROWS - GROUP :].astype(F32)
+            shift = tail_rows[SHIFT_ROW : SHIFT_ROW + 1]
+            for group in range(N_CP):
+                here = pl.ds(group * count, count)
+                projected = jnp.dot(coefs[here, :], stacked, preferred_element_type=F32)
+                for half in range(2):
+                    side = slice(half * LANES, (half + 1) * LANES)
+                    to = (pair * 2 + half) * LANES
+                    part = projected[:, side] * scales[here, :] + shift[:, side]
+                    if which < 2:
+                        power = jnp.sum(part * part, axis=1, keepdims=True) * (1.0 / HD)
+                        part = part * lax.rsqrt(power + 1e-06)
+                        part = part * gain[which : which + 1, to : to + LANES]
+                    results[which, here, to : to + LANES] = part.astype(BF16)
+                if pair == 2:
+                    write = pltpu.make_async_copy(
+                        results.at[which, here], out.at[here], result_sems.at[which, group]
+                    )
+                    write.start()
+                    writes.append(write)
+    for write in writes:
+        write.wait()
+
+
+def project(panel, coefs, scales, gain):
+    tokens = coefs.shape[0]
+    out = jax.ShapeDtypeStruct((tokens, gain.shape[1]), BF16)
+    return pl.pallas_call(
+        project_kernel,
+        out_shape=(out, out, out),
+        in_specs=[pl.BlockSpec(memory_space=pltpu.VMEM)] * 4,
+        out_specs=(pl.BlockSpec(memory_space=pltpu.HBM),) * 3,
+        scratch_shapes=[
+            pltpu.VMEM((3, tokens, gain.shape[1]), BF16),
+            pltpu.SemaphoreType.DMA((3, N_CP)),
+        ],
+        compiler_params=pltpu.CompilerParams(vmem_limit_bytes=32 * 1024 * 1024),
+    )(panel, coefs, scales, gain)
 
 
 def body(
@@ -675,7 +705,7 @@
     qkv_weight,
     qk_gain,
 ):
-    results = exchange(
+    panel, coefs, scales = exchange(
         video.reshape(-1, C),
         conv_weight,
         conv_bias.reshape(1, -1),
@@ -690,9 +720,8 @@
         col_pos,
         modulation,
         qkv_weight,
-        qk_gain,
     )
-    return results
+    return project(panel, coefs, scales, qk_gain)
 
 
 def solution(mesh):

time: 37.1 us -> 35.7 us (0.962)
  local copies, waits for them, and re-layouts: 2.74 us -> 0.01 us
  Pallas kernels: 33.6 us -> 34.9 us
    unnamed x3 -> x2, local copies, waits for them, and re-layouts: 2.74 us -> 0.01 us
    pallas_call x1 -> x2, Pallas kernels: 33.6 us -> 34.9 us  [the longest x1 32.3 us: exchange(): pl.pallas_call(exchange_kernel, out_shape=(jax.ShapeDtypeStruct((2 * RING...]
where the time goes in v5:
time: 35.7 us; the launch traced here: 35.6 us
  Pallas kernels  34.9 us (98%)
  between operations  0.66 us (2%)
    pallas_call x1, Pallas kernels, exchange(): pl.pallas_call(exchange_kernel, out_shape=(jax.ShapeDtypeStruct((2 * RING...  32.3 us
    pallas_call x1, Pallas kernels, project(): pl.pallas_call(project_kernel, out_shape=(out, out, out), in_specs=[pl.Bl...  2.59 us

profile of v5, /device:TPU:0, one launch (start us, length us, event | category | flops | bytes accessed | tf_op | source)
XLA Modules:
  0.0 35.6 jit_solution(11677945181830189591)
XLA Ops:
  0.6 0.0 copy-start
  0.6 32.3 %shard_map.166 = (bf16[200,16,128]{2,1,0:T(8,128)(2,1)S(1)}, bf16[576,240]{1,0:T(8,128)(2,1)S(1)}, f32[576,128]{1,0:T(8,128)S(1)}) custom-call(bf16[1152,512]{1,0:T(8,128)(2,1)} %bitcast.6, bf16[3,3,512,512]{3,2,1,0:T(8,128)(2,1)} %conv_far.1, f32[1,512]{1,0:T(1,128)} %bitcast.9, bf16[3,512,512]{2,1,0:T(8,128)(2,1)} %time_far.1, f32[1,512]{1,0:T(1,128)} %bitcast.10, ...), custom_call_target="tpu_custom_call" | custom-call | tf_op jit(solution)/shard_map/pallas_call | solution.py:574
  33.0 0.0 copy-done
  33.0 2.6 %shard_map.167 = (bf16[576,768]{1,0:T(8,128)(2,1)}, bf16[576,768]{1,0:T(8,128)(2,1)}, bf16[576,768]{1,0:T(8,128)(2,1)}) custom-call(bf16[200,16,128]{2,1,0:T(8,128)(2,1)S(1)} %get-tuple-element.6.panel, bf16[576,240]{1,0:T(8,128)(2,1)S(1)} %get-tuple-element.7.coefs, f32[576,128]{1,0:T(8,128)S(1)} %get-tuple-element.8.scales, f32[2,768]{1,0:T(2,128)S(1)} %copy-done), custom_call_target="tpu_custom_call" | custom-call | tf_op jit(solution)/shard_map/pallas_call | solution.py:678
Async XLA Ops:
  0.6 32.4 %copy-start = (f32[2,768]{1,0:T(2,128)S(1)}, f32[2,768]{1,0:T(2,128)}, u32[]{:S(2)}) copy-start(f32[2,768]{1,0:T(2,128)} %gain.1) | copy-start | bytes 18436

commit v6 on v5

--- a/solution.py
+++ b/solution.py
@@ -39,9 +39,10 @@
 HEAD_TILES = 18
 HALF_TILES = HEAD_TILES // 2 * GROUPS
 QUARTER = 25
-SMALL = 4
+SMALL = 3
 RING = 4
 NEAR = 8
+LAST = NEAR * SMALL
 CELL_ROWS = 80
 CHUNK = 4 * 96
 OWN = D // N_FSDP
@@ -116,7 +117,9 @@
     ring_in,
     blocks,
     near_in,
+    last_in,
     pieces,
+    lasts,
     gathered,
     folded,
     kernels,
@@ -138,6 +141,7 @@
     ring_sems,
     near_sems,
     spread_sems,
+    last_sems,
     panel_sems,
     edge_send,
     edge_recv,
@@ -357,9 +361,7 @@
         total = parts[half, pl.ds(ring_at[half] * QUARTER, QUARTER)].astype(F32)
         for other in range(RING - 1):
             total = total + ring_in[half, other].astype(F32)
-        blocks[half, pl.ds(0, QUARTER)] = total.astype(BF16)
-        spare = NEAR * SMALL - QUARTER
-        blocks[half, pl.ds(QUARTER, spare)] = jnp.zeros((spare, GROUP, LANES), BF16)
+        blocks[half] = total.astype(BF16)
         for slot, step in enumerate(near_steps):
             target, peer = near_peer(half, step)
             pltpu.make_async_remote_copy(
@@ -370,6 +372,18 @@
                 device_id={"fsdp": peer},
                 device_id_type=MESH,
             ).start()
+
+            @pl.when(target == 0)
+            def _():
+                pltpu.make_async_remote_copy(
+                    src_ref=blocks.at[half, pl.ds(LAST, 1)],
+                    dst_ref=last_in.at[half, slot],
+                    send_sem=last_sems.at[half],
+                    recv_sem=last_sems.at[2 + half],
+                    device_id={"fsdp": peer},
+                    device_id_type=MESH,
+                ).start()
+
     empty = jnp.zeros((2 * WIDE, LANES), F32)
     padded[pl.ds(0, 2 * WIDE), :] = empty
     padded[pl.ds((ROWS + 2) * WIDE, 2 * WIDE), :] = empty
@@ -453,7 +467,6 @@
         for other in range(NEAR - 1):
             total = total + near_in[half, other].astype(F32)
         pieces[half] = total.astype(BF16)
-        gathered[half, pl.ds(near_at(half) * SMALL, SMALL)] = pieces[half]
         for step in near_steps:
             pltpu.make_async_remote_copy(
                 src_ref=pieces.at[half],
@@ -463,6 +476,25 @@
                 device_id={"fsdp": near_peer(half, step)[1]},
                 device_id_type=MESH,
             ).start()
+        gathered[half, pl.ds(near_at(half) * SMALL, SMALL)] = pieces[half]
+
+        @pl.when(near_at(half) == 0)
+        def _():
+            wait_bytes(last_in.at[half], last_sems.at[2 + half])
+            total = blocks[half, pl.ds(LAST, 1)].astype(F32)
+            for other in range(NEAR - 1):
+                total = total + last_in[half, other].astype(F32)
+            lasts[half] = total.astype(BF16)
+            for step in near_steps:
+                pltpu.make_async_remote_copy(
+                    src_ref=lasts.at[half],
+                    dst_ref=gathered.at[half, pl.ds(LAST, 1)],
+                    send_sem=last_sems.at[4 + half],
+                    recv_sem=last_sems.at[6 + half],
+                    device_id={"fsdp": near_peer(half, step)[1]},
+                    device_id_type=MESH,
+                ).start()
+            gathered[half, pl.ds(LAST, 1)] = lasts[half]
 
     loads[14].wait()
     centers[pl.ds(0, PW_ROWS), :] = centers[pl.ds(PW_ROWS, PW_ROWS), :]
@@ -482,6 +514,11 @@
     panel_copies = []
     for half in range(2):
         wait_bytes(gathered.at[half, pl.ds(0, (NEAR - 1) * SMALL)], spread_sems.at[2 + half])
+
+        @pl.when(near_at(half) != 0)
+        def _():
+            wait_bytes(gathered.at[half, pl.ds(LAST, 1)], last_sems.at[6 + half])
+
         at = half * RING * QUARTER + ring_at[half] * QUARTER
         for step in (2, 1, 3):
             panel_copies.append(
@@ -565,6 +602,14 @@
         wait_bytes(gathered.at[half, pl.ds(0, (NEAR - 1) * SMALL)], spread_sems.at[half])
         wait_bytes(sent, panel_sems.at[half])
 
+        @pl.when(near_at(half) == 0)
+        def _():
+            wait_bytes(last_in.at[half], last_sems.at[4 + half])
+
+        @pl.when(near_at(half) != 0)
+        def _():
+            wait_bytes(last_in.at[half, 0], last_sems.at[half])
+
 
 def exchange(*args):
     whole = pl.BlockSpec(memory_space=pltpu.VMEM)
@@ -599,10 +644,12 @@
             pltpu.VMEM((2 * TABLE_ROWS, OWN), BF16),
             pltpu.VMEM((2, RING * QUARTER, GROUP, LANES), BF16),
             pltpu.VMEM((2, RING - 1, QUARTER, GROUP, LANES), BF16),
-            pltpu.VMEM((2, NEAR * SMALL, GROUP, LANES), BF16),
+            pltpu.VMEM((2, QUARTER, GROUP, LANES), BF16),
             pltpu.VMEM((2, NEAR - 1, SMALL, GROUP, LANES), BF16),
+            pltpu.VMEM((2, NEAR - 1, 1, GROUP, LANES), BF16),
             pltpu.VMEM((2, SMALL, GROUP, LANES), BF16),
-            pltpu.VMEM((2, NEAR * SMALL, GROUP, LANES), BF16),
+            pltpu.VMEM((2, 1, GROUP, LANES), BF16),
+            pltpu.VMEM((2, QUARTER, GROUP, LANES), BF16),
             pltpu.VMEM((C, 2 * LANES), BF16),
             pltpu.VMEM((3, C, 2 * LANES), BF16),
             pltpu.VMEM((pixels, LANES), F32),
@@ -623,6 +670,7 @@
             pltpu.SemaphoreType.DMA((4,)),
             pltpu.SemaphoreType.DMA((4,)),
             pltpu.SemaphoreType.DMA((4,)),
+            pltpu.SemaphoreType.DMA((8,)),
             pltpu.SemaphoreType.DMA((4,)),
             pltpu.SemaphoreType.DMA((2,)),
             pltpu.SemaphoreType.DMA((2,)),
@@ -636,23 +684,28 @@
 
 
 def project_kernel(
-    panel, coefs, scales, gain, query, keys, values, results, result_sems
+    panel, coefs, scales, gain, query, keys, values, stacked, results, result_sems
 ):
     count = 2 * CELLS
     writes = []
-    for which, out in enumerate((query, keys, values)):
+    for which, out in ((2, values), (0, query), (1, keys)):
+        pairs = []
         for pair in range(3):
             sides = []
             for head in range(which * 6 + pair * 2, which * 6 + pair * 2 + 2):
                 rows = panel[pl.ds(head // (HEAD_TILES // 2) + head * GROUPS, GROUPS)]
                 sides.append(rows.reshape(TABLE_ROWS, LANES))
             both = jnp.concatenate(sides, axis=1)
-            stacked = jnp.concatenate([both[:PW_ROWS], both], axis=0)
+            stacked[pair, pl.ds(0, PW_ROWS)] = both[:PW_ROWS]
+            stacked[pair, pl.ds(PW_ROWS, TABLE_ROWS)] = both
             tail_rows = both[TABLE_ROWS - GROUP :].astype(F32)
-            shift = tail_rows[SHIFT_ROW : SHIFT_ROW + 1]
-            for group in range(N_CP):
-                here = pl.ds(group * count, count)
-                projected = jnp.dot(coefs[here, :], stacked, preferred_element_type=F32)
+            pairs.append(tail_rows[SHIFT_ROW : SHIFT_ROW + 1])
+        for group in range(N_CP):
+            here = pl.ds(group * count, count)
+            for pair, shift in enumerate(pairs):
+                projected = jnp.dot(
+                    coefs[here, :], stacked[pair], preferred_element_type=F32
+                )
                 for half in range(2):
                     side = slice(half * LANES, (half + 1) * LANES)
                     to = (pair * 2 + half) * LANES
@@ -662,12 +715,11 @@
                         part = part * lax.rsqrt(power + 1e-06)
                         part = part * gain[which : which + 1, to : to + LANES]
                     results[which, here, to : to + LANES] = part.astype(BF16)
-                if pair == 2:
-                    write = pltpu.make_async_copy(
-                        results.at[which, here], out.at[here], result_sems.at[which, group]
-                    )
-                    write.start()
-                    writes.append(write)
+            write = pltpu.make_async_copy(
+                results.at[which, here], out.at[here], result_sems.at[which, group]
+            )
+            write.start()
+            writes.append(write)
     for write in writes:
         write.wait()
 
@@ -681,6 +733,7 @@
         in_specs=[pl.BlockSpec(memory_space=pltpu.VMEM)] * 4,
         out_specs=(pl.BlockSpec(memory_space=pltpu.HBM),) * 3,
         scratch_shapes=[
+            pltpu.VMEM((3, KEPT, 2 * LANES), BF16),
             pltpu.VMEM((3, tokens, gain.shape[1]), BF16),
             pltpu.SemaphoreType.DMA((3, N_CP)),
         ],

time: 35.7 us -> 34.8 us (0.975)
  Pallas kernels: 34.9 us -> 34 us
    pallas_call x1, Pallas kernels: 32.3 us -> 31.6 us  [exchange(): pl.pallas_call(exchange_kernel, out_shape=(jax.ShapeDtypeStruct((2 * RING...]
where the time goes in v6:
time: 34.8 us; the launch traced here: 34.6 us
  Pallas kernels  34 us (98%)
  between operations  0.66 us (2%)
    pallas_call x1, Pallas kernels, exchange(): pl.pallas_call(exchange_kernel, out_shape=(jax.ShapeDtypeStruct((2 * RING...  31.6 us
    pallas_call x1, Pallas kernels, project(): pl.pallas_call(project_kernel, out_shape=(out, out, out), in_specs=[pl.Bl...  2.33 us

profile of v6, /device:TPU:0, one launch (start us, length us, event | category | flops | bytes accessed | tf_op | source)
XLA Modules:
  0.0 34.6 jit_solution(5742006886148921954)
XLA Ops:
  0.6 0.0 copy-start
  0.6 31.6 %shard_map.166 = (bf16[200,16,128]{2,1,0:T(8,128)(2,1)S(1)}, bf16[576,240]{1,0:T(8,128)(2,1)S(1)}, f32[576,128]{1,0:T(8,128)S(1)}) custom-call(bf16[1152,512]{1,0:T(8,128)(2,1)} %bitcast.6, bf16[3,3,512,512]{3,2,1,0:T(8,128)(2,1)} %conv_far.1, f32[1,512]{1,0:T(1,128)} %bitcast.9, bf16[3,512,512]{2,1,0:T(8,128)(2,1)} %time_far.1, f32[1,512]{1,0:T(1,128)} %bitcast.10, ...), custom_call_target="tpu_custom_call" | custom-call | tf_op jit(solution)/shard_map/pallas_call | solution.py:619
  32.3 0.0 copy-done
  32.3 2.3 %shard_map.167 = (bf16[576,768]{1,0:T(8,128)(2,1)}, bf16[576,768]{1,0:T(8,128)(2,1)}, bf16[576,768]{1,0:T(8,128)(2,1)}) custom-call(bf16[200,16,128]{2,1,0:T(8,128)(2,1)S(1)} %get-tuple-element.6.panel, bf16[576,240]{1,0:T(8,128)(2,1)S(1)} %get-tuple-element.7.coefs, f32[576,128]{1,0:T(8,128)S(1)} %get-tuple-element.8.scales, f32[2,768]{1,0:T(2,128)S(1)} %copy-done), custom_call_target="tpu_custom_call" | custom-call | tf_op jit(solution)/shard_map/pallas_call | solution.py:730
Async XLA Ops:
  0.6 31.7 %copy-start = (f32[2,768]{1,0:T(2,128)S(1)}, f32[2,768]{1,0:T(2,128)}, u32[]{:S(2)}) copy-start(f32[2,768]{1,0:T(2,128)} %gain.1) | copy-start | bytes 18436

commit v7 on v6

--- a/solution.py
+++ b/solution.py
@@ -151,22 +151,23 @@
     me = lax.axis_index("fsdp")
     column = lax.axis_index("cp")
     barrier = pltpu.get_barrier_semaphore()
-    z_at, x_at, y_at = me // 8, me // 4 % 2, me % 4
+    z_at, x_at, y_at = lax.div(me, 8), lax.rem(lax.div(me, 4), 2), lax.rem(me, 4)
+    plane_at = lax.rem(me, 8)
 
     def ring_peer(half, step):
         if half == 0:
-            return (z_at + step) % RING * 8 + me % 8
-        return me // 4 * 4 + (y_at + step) % RING
+            return lax.rem(z_at + step, RING) * 8 + plane_at
+        return me - y_at + lax.rem(y_at + step, RING)
 
     def near_at(half):
-        return me % 8 if half == 0 else z_at * 2 + x_at
+        return plane_at if half == 0 else z_at * 2 + x_at
 
     def near_peer(half, step):
-        x_to = (x_at + step[0]) % 2
+        x_to = 1 - x_at if step[0] else x_at
         if half == 0:
-            ring_to = (y_at + step[1]) % RING
+            ring_to = lax.rem(y_at + step[1], RING)
             return x_to * RING + ring_to, z_at * 8 + x_to * 4 + ring_to
-        ring_to = (z_at + step[1]) % RING
+        ring_to = lax.rem(z_at + step[1], RING)
         return ring_to * 2 + x_to, ring_to * 8 + x_to * 4 + y_at
 
     near_steps = ((1, 2), (1, 1), (1, 3), (0, 2), (1, 0), (0, 1), (0, 3))
@@ -202,7 +203,10 @@
 
     def greet(step, carry):
         pl.semaphore_signal(
-            barrier, inc=1, device_id={"fsdp": (me + step) % N_FSDP}, device_id_type=MESH
+            barrier,
+            inc=1,
+            device_id={"fsdp": lax.rem(me + step, N_FSDP)},
+            device_id_type=MESH,
         )
         return carry
 
@@ -268,7 +272,7 @@
     ring_copies = []
     for step in (2, 1, 3):
         for half in range(2):
-            target = (ring_at[half] + step) % RING
+            target = lax.rem(ring_at[half] + step, RING)
             ring_copies.append(
                 pltpu.make_async_remote_copy(
                     src_ref=parts.at[half, pl.ds(target * QUARTER, QUARTER)],
@@ -417,7 +421,7 @@
         )
         if 0 <= row < ROWS:
             total = total + direct[pl.ds(row * WIDE, WIDE), :]
-        spread_out[...] = jnp.where(own_lanes, total, 0.0)
+        spread_out[pl.ds(0, WIDE), :] = jnp.where(own_lanes, total, 0.0)
         result = None
         for side in range(2):
             taken = spread_out[pl.ds(side, WIDE // 2, stride=2), :]
@@ -444,7 +448,7 @@
     slot = (me + N_FSDP - 4) % N_FSDP
 
     def tile_copy(step):
-        target = (me + step) % N_FSDP
+        target = lax.rem(me + step, N_FSDP)
         return pltpu.make_async_remote_copy(
             src_ref=messages.at[target],
             dst_ref=latents_in.at[slot],
@@ -652,14 +656,14 @@
             pltpu.VMEM((2, QUARTER, GROUP, LANES), BF16),
             pltpu.VMEM((C, 2 * LANES), BF16),
             pltpu.VMEM((3, C, 2 * LANES), BF16),
-            pltpu.VMEM((pixels, LANES), F32),
-            pltpu.VMEM((pixels, LANES), F32),
-            pltpu.VMEM((pixels, LANES), F32),
-            pltpu.VMEM((pixels, LANES), F32),
+            pltpu.VMEM((pixels + COLS, LANES), F32),
+            pltpu.VMEM((pixels + COLS, LANES), F32),
+            pltpu.VMEM((pixels + COLS, LANES), F32),
+            pltpu.VMEM((pixels + COLS, LANES), F32),
             pltpu.VMEM((2, ROWS * WINDOWS, LANES), F32),
             pltpu.VMEM((2, ROWS * WINDOWS, LANES), F32),
             pltpu.VMEM(((ROWS + 4) * WIDE, LANES), F32),
-            pltpu.VMEM((WIDE, LANES), F32),
+            pltpu.VMEM((WIDE + 8, LANES), F32),
             pltpu.VMEM((N_FSDP, GROUP, LANES), F32),
             pltpu.VMEM((N_FSDP, GROUP, LANES), BF16),
             pltpu.VMEM((N_FSDP, GROUP, LANES), BF16),

time: 34.8 us -> 34.8 us (level)
  no operation moved by 1% of the time
where the time goes in v7:
time: 34.8 us; the launch traced here: 34.6 us
  Pallas kernels  34 us (98%)
  between operations  0.66 us (2%)
    pallas_call x1, Pallas kernels, exchange(): pl.pallas_call(exchange_kernel, out_shape=(jax.ShapeDtypeStruct((2 * RING...  31.6 us
    pallas_call x1, Pallas kernels, project(): pl.pallas_call(project_kernel, out_shape=(out, out, out), in_specs=[pl.Bl...  2.34 us

profile of v7, /device:TPU:0, one launch (start us, length us, event | category | flops | bytes accessed | tf_op | source)
XLA Modules:
  0.0 34.6 jit_solution(6743925718705145062)
XLA Ops:
  0.6 0.0 copy-start
  0.6 31.6 %shard_map.166 = (bf16[200,16,128]{2,1,0:T(8,128)(2,1)S(1)}, bf16[576,240]{1,0:T(8,128)(2,1)S(1)}, f32[576,128]{1,0:T(8,128)S(1)}) custom-call(bf16[1152,512]{1,0:T(8,128)(2,1)} %bitcast.6, bf16[3,3,512,512]{3,2,1,0:T(8,128)(2,1)} %conv_far.1, f32[1,512]{1,0:T(1,128)} %bitcast.9, bf16[3,512,512]{2,1,0:T(8,128)(2,1)} %time_far.1, f32[1,512]{1,0:T(1,128)} %bitcast.10, ...), custom_call_target="tpu_custom_call" | custom-call | tf_op jit(solution)/shard_map/pallas_call | solution.py:623
  32.3 0.0 copy-done
  32.3 2.3 %shard_map.167 = (bf16[576,768]{1,0:T(8,128)(2,1)}, bf16[576,768]{1,0:T(8,128)(2,1)}, bf16[576,768]{1,0:T(8,128)(2,1)}) custom-call(bf16[200,16,128]{2,1,0:T(8,128)(2,1)S(1)} %get-tuple-element.6.panel, bf16[576,240]{1,0:T(8,128)(2,1)S(1)} %get-tuple-element.7.coefs, f32[576,128]{1,0:T(8,128)S(1)} %get-tuple-element.8.scales, f32[2,768]{1,0:T(2,128)S(1)} %copy-done), custom_call_target="tpu_custom_call" | custom-call | tf_op jit(solution)/shard_map/pallas_call | solution.py:734
Async XLA Ops:
  0.6 31.7 %copy-start = (f32[2,768]{1,0:T(2,128)S(1)}, f32[2,768]{1,0:T(2,128)}, u32[]{:S(2)}) copy-start(f32[2,768]{1,0:T(2,128)} %gain.1) | copy-start | bytes 18436

commit v8 on v7

--- a/solution.py
+++ b/solution.py
@@ -215,7 +215,7 @@
         pl.semaphore_signal(
             barrier, inc=1, device_id={"cp": (column + step) % N_CP}, device_id_type=MESH
         )
-    for load in loads[:7]:
+    for load in loads[3:6]:
         load.wait()
     bias = patch_bias[...]
     bias_high = bias.astype(BF16).astype(F32)
@@ -238,6 +238,8 @@
 
     for group in range(GROUPS):
         at = PW_ROWS + group * GROUP
+        if group in (0, 4, 7):
+            loads[(0, 4, 7).index(group)].wait()
         whole = tables[pl.ds(at, GROUP), :].astype(F32)
         center = jnp.sum(whole, axis=1, keepdims=True) * (1.0 / D)
         centers[pl.ds(at, GROUP), :] = jnp.broadcast_to(center, (GROUP, LANES))
@@ -250,6 +252,7 @@
         high, low = split_2(block)
         left_side[pl.ds(group * GROUP, GROUP), :] = high
         left_side[pl.ds(TABLE_ROWS + group * GROUP, GROUP), :] = low
+    loads[6].wait()
     for which in range(3):
         for pair in range(3):
             part = jnp.dot(

time: 34.8 us -> 34.7 us (level)
  no operation moved by 1% of the time
where the time goes in v8:
time: 34.7 us; the launch traced here: 34.6 us
  Pallas kernels  34 us (98%)
  between operations  0.66 us (2%)
    pallas_call x1, Pallas kernels, exchange(): pl.pallas_call(exchange_kernel, out_shape=(jax.ShapeDtypeStruct((2 * RING...  31.6 us
    pallas_call x1, Pallas kernels, project(): pl.pallas_call(project_kernel, out_shape=(out, out, out), in_specs=[pl.Bl...  2.34 us

profile of v8, /device:TPU:0, one launch (start us, length us, event | category | flops | bytes accessed | tf_op | source)
XLA Modules:
  0.0 34.6 jit_solution(12690481495328177403)
XLA Ops:
  0.6 0.0 copy-start
  0.6 31.6 %shard_map.166 = (bf16[200,16,128]{2,1,0:T(8,128)(2,1)S(1)}, bf16[576,240]{1,0:T(8,128)(2,1)S(1)}, f32[576,128]{1,0:T(8,128)S(1)}) custom-call(bf16[1152,512]{1,0:T(8,128)(2,1)} %bitcast.6, bf16[3,3,512,512]{3,2,1,0:T(8,128)(2,1)} %conv_far.1, f32[1,512]{1,0:T(1,128)} %bitcast.9, bf16[3,512,512]{2,1,0:T(8,128)(2,1)} %time_far.1, f32[1,512]{1,0:T(1,128)} %bitcast.10, ...), custom_call_target="tpu_custom_call" | custom-call | tf_op jit(solution)/shard_map/pallas_call | solution.py:626
  32.3 0.0 copy-done
  32.3 2.3 %shard_map.167 = (bf16[576,768]{1,0:T(8,128)(2,1)}, bf16[576,768]{1,0:T(8,128)(2,1)}, bf16[576,768]{1,0:T(8,128)(2,1)}) custom-call(bf16[200,16,128]{2,1,0:T(8,128)(2,1)S(1)} %get-tuple-element.6.panel, bf16[576,240]{1,0:T(8,128)(2,1)S(1)} %get-tuple-element.7.coefs, f32[576,128]{1,0:T(8,128)S(1)} %get-tuple-element.8.scales, f32[2,768]{1,0:T(2,128)S(1)} %copy-done), custom_call_target="tpu_custom_call" | custom-call | tf_op jit(solution)/shard_map/pallas_call | solution.py:737
Async XLA Ops:
  0.6 31.6 %copy-start = (f32[2,768]{1,0:T(2,128)S(1)}, f32[2,768]{1,0:T(2,128)}, u32[]{:S(2)}) copy-start(f32[2,768]{1,0:T(2,128)} %gain.1) | copy-start | bytes 18436
